TPU v7x, 32 devices: a whole 2x2x4 slice. The times are simulated.
32 devices in a mesh: head: 4 (over y, x), blk: 8 (over z, core).
Axes of the slice: x: 2, y: 2, z: 4, core: 2. Of those that a mesh axis runs over, the one named last changes fastest.
Arguments:
- tokens: bfloat16 [512, 2048], P('blk'), may hold values from -6 to 6
- q_weight: bfloat16 [2048, 1024], P(None, 'head')
- k_weight: bfloat16 [2048, 256], P(None, 'head')
- v_weight: bfloat16 [2048, 256], P(None, 'head'), may hold values from -0.125 to 0.125
- o_weight: bfloat16 [1024, 2048], P('head'), may hold values from -0.1875 to 0.1875
- kv_pages: bfloat16 [4, 24, 64, 128], P('head', 'blk')
- page_node: int32 [24], replicated, may hold values from 0 to 12, as said below
- page_fill: int32 [24], replicated, may hold values from 1 to 64
- req_len: int32 [4], replicated, may hold values from 1 to 256, 512 in all
- req_leaf: int32 [4], replicated, may hold values from 0 to 3
- leaf_parent: int32 [4], replicated, may hold values from 0 to 7
Outputs:
- attn_out: bfloat16 [512, 2048], P('blk', 'head')
Inputs may be any that keep to these rules, and one draw needn't show every extreme that they name: `req_len`: their sum is 512, and the longest request has exactly 256 tokens. `page_node`: node 0 is the root, nodes 1 to 8 form the middle level and the rest are leaves; the root holds a third of the 24 pages, each middle node a 1 / 8 share of another third, each leaf two pages, placed over the pages in any order.
All inputs are finite; a program needn't handle non-finite values.
Results may differ from a plain program's by a relative error of at most 0.012.
The roundings to bfloat16 on the way count: a program that leaves them out, or rounds other values in their place, can miss the bound.
Values may be sent and summed in bfloat16 or wider, within the bound.
No kernel may reach another device: no remote copies, remote signals or barrier semaphores. Data moves between devices by JAX's collectives and lax.ppermute only.
A program may use at most 128 MiB of HBM per device.

v0:
```python
import jax
import jax.numpy as jnp
from jax import lax
from jax.sharding import PartitionSpec as P

HD = 64
MIDS = 8
PROMPT = 256


NEGATIVE = -1e30
EPSILON = 1e-06
ROPE_BASE = 10000.0
SCORE_SCALE = 0.125


def shifted(value, axis, steps):
    count = lax.axis_size(axis)
    first, last = (max(0, -steps), min(count, count - steps))
    return lax.ppermute(value, axis, [(source, source + steps) for source in range(first, last)])


def norm_rows(hidden):
    wide = hidden.astype(jnp.float32)
    return (wide * lax.rsqrt(jnp.mean(wide * wide, axis=-1, keepdims=True) + EPSILON)).astype(
        jnp.bfloat16
    )


def rotate(values, positions):
    half_dim = values.shape[-1] // 2
    frequency = ROPE_BASE ** (-jnp.arange(half_dim).astype(jnp.float32) / half_dim)
    angles = positions.astype(jnp.float32)[:, None] * frequency[None, :]
    cosine = jnp.cos(angles)[:, None, :]
    sine_part = jnp.sin(angles)[:, None, :]
    first_half = values[..., :half_dim]
    second = values[..., half_dim:]
    return jnp.concatenate(
        [first_half * cosine - second * sine_part, second * cosine + first_half * sine_part],
        axis=-1,
    )


def request_of(places, req_len):
    req_end = jnp.cumsum(req_len)
    return jnp.sum((places[:, None] >= req_end[None, :]).astype(jnp.int32), axis=1)


def row_paths(places, req_len, req_leaf, leaf_parent, page_node, page_fill):
    req_count = req_len.shape[0]
    leaf_count = leaf_parent.shape[0]
    node_count = 1 + MIDS + leaf_count
    starts = jnp.cumsum(req_len) - req_len
    request = request_of(places, req_len)
    chosen = request[:, None] == jnp.arange(req_count, dtype=jnp.int32)[None, :]
    offset = places - jnp.sum(jnp.where(chosen, starts[None, :], 0), axis=1)
    leaf_id = jnp.sum(jnp.where(chosen, req_leaf[None, :], 0), axis=1)
    leaf_hit = leaf_id[:, None] == jnp.arange(leaf_count, dtype=jnp.int32)[None, :]
    mid_id = jnp.sum(jnp.where(leaf_hit, leaf_parent[None, :], 0), axis=1)
    path_ids = jnp.stack([jnp.zeros_like(mid_id), 1 + mid_id, 1 + MIDS + leaf_id], axis=1)
    node_hit = page_node[:, None] == jnp.arange(node_count, dtype=jnp.int32)[None, :]
    node_len = jnp.sum(jnp.where(node_hit, page_fill[:, None], 0), axis=0)
    on_path = path_ids[:, :, None] == jnp.arange(node_count, dtype=jnp.int32)[None, None, :]
    prefix = jnp.sum(jnp.where(on_path, node_len[None, None, :], 0), axis=(1, 2))
    return (request, path_ids, prefix + offset)


def page_mask(path_ids, nodes_here, fills_here, page_len):
    node_hit = jnp.any(path_ids[:, :, None] == nodes_here[None, None, :], axis=1)
    slot_live = jnp.arange(page_len, dtype=jnp.int32)[None, :] < fills_here[:, None]
    return (node_hit[:, :, None] & slot_live[None, :, :]).reshape(path_ids.shape[0], -1)


def block_size(total_pages, page_limit):
    chosen = 1
    for trial_size in range(1, min(total_pages, page_limit) + 1):
        if total_pages % trial_size == 0:
            chosen = trial_size
    return chosen


def fold_keys(running, q_rot, key_rows, values, allowed):
    top_old, total_old, accum_old = running
    scores = (
        jnp.einsum("rkhd,knd->khrn", q_rot, key_rows, preferred_element_type=jnp.float32)
        * SCORE_SCALE
    )
    scores = jnp.where(allowed[None, None], scores, NEGATIVE)
    top_new = jnp.maximum(top_old, jnp.max(scores, axis=-1))
    weights = jnp.where(allowed[None, None], jnp.exp(scores - top_new[..., None]), 0.0)
    factor = jnp.exp(top_old - top_new)
    total_new = total_old * factor + jnp.sum(weights, axis=-1)
    product = jnp.einsum(
        "khrn,knd->khrd", weights.astype(jnp.bfloat16), values, preferred_element_type=jnp.float32
    )
    return (top_new, total_new, accum_old * factor[..., None] + product)


def local(
    tokens,
    q_weight,
    k_weight,
    v_weight,
    o_weight,
    kv_pages,
    page_node,
    page_fill,
    req_len,
    req_leaf,
    leaf_parent,
):
    local_rows = tokens.shape[0]
    kv_heads = k_weight.shape[1] // HD
    q_heads = q_weight.shape[1] // HD
    group_size = q_heads // kv_heads
    page_len = kv_pages.shape[2]
    blk_index = lax.axis_index("blk")
    places = blk_index * local_rows + jnp.arange(local_rows, dtype=jnp.int32)
    request, path_ids, positions = row_paths(
        places, req_len, req_leaf, leaf_parent, page_node, page_fill
    )
    normed = norm_rows(tokens)
    queries = jnp.dot(normed, q_weight, preferred_element_type=jnp.float32).reshape(
        local_rows, q_heads, HD
    )
    q_rot = (
        rotate(queries, positions)
        .astype(jnp.bfloat16)
        .reshape(local_rows, kv_heads, group_size, HD)
    )
    keys_new = jnp.dot(normed, k_weight, preferred_element_type=jnp.float32).reshape(
        local_rows, kv_heads, HD
    )
    keys_new = rotate(keys_new, positions).astype(jnp.bfloat16)
    values_new = (
        jnp.dot(normed, v_weight, preferred_element_type=jnp.float32)
        .astype(jnp.bfloat16)
        .reshape(local_rows, kv_heads, HD)
    )
    own_pack = jnp.concatenate([keys_new, values_new], axis=-1)
    reach_devs = (PROMPT - 1) // local_rows + 1
    near_packs = [own_pack]
    near_places = [places]
    for distance in range(1, reach_devs + 1):
        near_packs.insert(0, shifted(own_pack, "blk", distance))
        near_places.insert(0, places - distance * local_rows)
    near_pack = jnp.swapaxes(jnp.concatenate(near_packs, axis=0), 0, 1)
    near_place = jnp.concatenate(near_places)
    near_req = request_of(jnp.maximum(near_place, 0), req_len)
    near_ok = (
        (near_place[None, :] >= 0)
        & (near_req[None, :] == request[:, None])
        & (near_place[None, :] <= places[:, None])
    )
    start_state = (
        jnp.full((kv_heads, group_size, local_rows), NEGATIVE, jnp.float32),
        jnp.zeros((kv_heads, group_size, local_rows), jnp.float32),
        jnp.zeros((kv_heads, group_size, local_rows, HD), jnp.float32),
    )
    running = fold_keys(start_state, q_rot, near_pack[..., :HD], near_pack[..., HD:], near_ok)
    group_limit = max(1, 2048 // page_len)
    shard_pages = lax.all_gather(kv_pages, "blk", axis=1, tiled=True)
    page_total = shard_pages.shape[1]
    group_pages = block_size(page_total, group_limit)

    def one_group(group_index, inner):
        first_page = group_index * group_pages
        page_block = lax.dynamic_slice_in_dim(shard_pages, first_page, group_pages, 1)
        nodes_here = lax.dynamic_slice_in_dim(page_node, first_page, group_pages, 0)
        fills_here = lax.dynamic_slice_in_dim(page_fill, first_page, group_pages, 0)
        allowed = page_mask(path_ids, nodes_here, fills_here, page_len)
        flat_block = page_block.reshape(kv_heads, group_pages * page_len, 2 * HD)
        return fold_keys(inner, q_rot, flat_block[..., :HD], flat_block[..., HD:], allowed)

    running = lax.fori_loop(0, page_total // group_pages, one_group, running)
    top_all, total_all, accum_all = running
    attended = accum_all / total_all[..., None]
    attended = (
        jnp.transpose(attended, (2, 0, 1, 3)).reshape(local_rows, q_heads * HD).astype(jnp.bfloat16)
    )
    partial_out = jnp.dot(attended, o_weight, preferred_element_type=jnp.float32)
    return lax.psum_scatter(partial_out, "head", scatter_dimension=1, tiled=True).astype(
        jnp.bfloat16
    )


def solution(mesh):
    return jax.shard_map(
        local,
        mesh=mesh,
        in_specs=(
            P("blk", None),
            P(None, "head"),
            P(None, "head"),
            P(None, "head"),
            P("head", None),
            P("head", "blk", None, None),
            P(),
            P(),
            P(),
            P(),
            P(),
        ),
        out_specs=P("blk", "head"),
        check_vma=False,
    )
```

profile of v0, /device:TPU:0, one launch (start us, length us, event | category | flops | bytes accessed | tf_op | source)
XLA Modules:
  0.0 80.6 jit_solution(4743349200905453745)
XLA Ops:
  6.5 0.0 copy-start
  6.5 0.0 copy-start.1
  6.5 0.0 copy-start.4
  6.5 0.0 copy-start.5
  6.5 0.0 copy-start.2
  6.5 0.0 reduce-scatter.2.cloned.1.call-start
  6.6 1.0 %reduce-window.8 = s32[4,1]{0,1:T(1,128)S(1)} reduce-window(s32[4,1]{0,1:T(1,128)} %bitcast.77, s32[]{:T(128)} %constant.28.clone.1), window={size=4x1 pad=3_0x0_0}, to_apply=%region_0.0 | reduce-window | flops 12 | bytes 36 | tf_op jit(solution)/shard_map/reduce-window.3
  7.6 0.7 bitcast_subtract_fusion
  8.3 1.1 %fusion.16 = f32[64]{0:T(128)S(1)} fusion(bf16[64,2048]{1,0:T(8,128)(2,1)} %param.11), kind=kLoop, calls=%fused_computation.24 | loop fusion | flops 393152 | bytes 262400 | tf_op jit(solution)/shard_map/reduce_sum | solution.py:25
  9.4 0.1 convert_reduce_fusion.1
  9.5 0.7 select_reduce_fusion.2
  10.2 0.7 select_reduce_fusion.3
  11.0 1.3 %fusion.10 = bf16[64,1,64]{2,0,1:T(8,128)(2,1)S(1)} fusion(bf16[2048,64]{0,1:T(8,128)(2,1)} %param.14, bf16[64,2048]{1,0:T(8,128)(2,1)} %param.11, f32[64]{0:T(128)S(1)} %add_rsqrt_fusion), kind=kOutput, calls=%fused_computation.17 | convolution fusion | flops 17174528 | bytes 532736 | tf_op jit(solution)/shard_map/dot_general | solution.py:136
  12.3 1.3 %convolution_bitcast_fusion = f32[64,1,64]{0,2,1:T(8,128)S(1)} fusion(bf16[2048,64]{0,1:T(8,128)(2,1)} %param.13, bf16[64,2048]{1,0:T(8,128)(2,1)} %param.11, f32[64]{0:T(128)S(1)} %add_rsqrt_fusion), kind=kOutput, calls=%fused_computation.15 | convolution fusion | flops 17170432 | bytes 540928 | tf_op jit(solution)/shard_map/dot_general | solution.py:131
  13.6 0.0 copy-start.3
  13.6 0.8 select_reduce_fusion.1
  14.4 0.1 pad_add_fusion
  14.5 0.1 select_reduce_fusion
  14.6 0.1 fusion.30
  14.8 0.1 copy.44
  14.9 0.1 copy.45
  15.0 0.1 pad_maximum_fusion.1
  15.1 2.4 %collective-permute-start.3 = (bf16[64,1,128]{2,0,1:T(8,128)(2,1)S(1)}, bf16[64,1,128]{2,0,1:T(8,128)(2,1)S(1)}, u32[]{:S(2)}, u32[]{:S(2)}) collective-permute-start(bf16[64,1,128]{2,0,1:T(8,128)(2,1)S(1)} %pad_maximum_fusion.1), channel_id=1, source_target_pairs={{0,1},{1,2},{2,3},{3,4},{4,5},{5,6},{6,7},{8,9},{9,10},{10,11},{11... | collective-permute-start | bytes 49160 | tf_op jit(solution)/shard_map/ppermute | solution.py:20
  17.4 4.5 %collective-permute-start.2 = (bf16[64,1,128]{2,0,1:T(8,128)(2,1)S(1)}, bf16[64,1,128]{2,0,1:T(8,128)(2,1)S(1)}, u32[]{:S(2)}, u32[]{:S(2)}) collective-permute-start(bf16[64,1,128]{2,0,1:T(8,128)(2,1)S(1)} %pad_maximum_fusion.1), channel_id=1, source_target_pairs={{0,2},{1,3},{2,4},{3,5},{4,6},{5,7},{8,10},{9,11},{10,12},{11,13},... | collective-permute-start | bytes 49160 | tf_op jit(solution)/shard_map/ppermute | solution.py:20
  21.9 4.5 %collective-permute-start.1 = (bf16[64,1,128]{2,0,1:T(8,128)(2,1)S(1)}, bf16[64,1,128]{2,0,1:T(8,128)(2,1)S(1)}, u32[]{:S(2)}, u32[]{:S(2)}) collective-permute-start(bf16[64,1,128]{2,0,1:T(8,128)(2,1)S(1)} %pad_maximum_fusion.1), channel_id=1, source_target_pairs={{0,3},{1,4},{2,5},{3,6},{4,7},{8,11},{9,12},{10,13},{11,14},{12,15... | collective-permute-start | bytes 49160 | tf_op jit(solution)/shard_map/ppermute | solution.py:20
  26.4 1.9 %collective-permute-start = (bf16[64,1,128]{2,0,1:T(8,128)(2,1)S(1)}, bf16[64,1,128]{2,0,1:T(8,128)(2,1)S(1)}, u32[]{:S(2)}, u32[]{:S(2)}) collective-permute-start(bf16[64,1,128]{2,0,1:T(8,128)(2,1)S(1)} %pad_maximum_fusion.1), channel_id=1, source_target_pairs={{0,4},{1,5},{2,6},{3,7},{8,12},{9,13},{10,14},{11,15},{16,20},{17,... | collective-permute-start | bytes 49160 | tf_op jit(solution)/shard_map/ppermute | solution.py:20
  28.4 0.0 copy-done.5
  28.4 0.1 compare_reduce_fusion
  28.5 0.1 concatenate.35
  28.6 0.0 copy-done.4
  28.6 0.1 broadcast_reduce_fusion
  28.7 0.2 multiply_cosine_fusion
  28.9 0.1 convert_reduce_fusion
  29.0 0.1 copy.50
  29.1 0.1 lt.36
  29.1 0.1 lt.34
  29.2 0.0 copy-done.1
  29.2 0.0 copy-done.2
  29.2 0.3 fusion.38
  29.6 0.1 reshape.510
  29.7 0.1 fusion.42
  29.8 0.3 and.49
  30.1 0.3 and.50
  30.4 0.0 copy-done.3
  30.4 14.6 %all_gather.3 = bf16[1,24,64,128]{3,2,0,1:T(8,128)(2,1)S(1)} all-gather(bf16[1,3,64,128]{3,2,0,1:T(8,128)(2,1)S(1)} %bitcast.74), channel_id=1, replica_groups=mesh['head'=4,'blk'=8] {'blk'}, dimensions={1}, use_global_device_ids=true | all-gather | bytes 442368 | tf_op jit(solution)/shard_map/all_gather | solution.py:162
  45.0 0.1 broadcast_and_fusion
  45.1 0.5 fusion.44
  45.6 0.1 compare_and_fusion
  45.7 0.0 collective-permute-done
  45.7 0.0 collective-permute-done.1
  45.8 0.0 collective-permute-done.2
  45.8 0.0 collective-permute-done.3
  45.8 0.3 fusion.43
  46.2 0.4 fusion.2
  46.6 0.2 fusion.18
  46.9 0.3 fusion.7
  47.2 0.5 fusion.9
  47.7 0.1 copy.54
  47.7 0.1 convert_element_type.80
  47.9 0.0 copy-done
  47.9 1.1 %fusion.45 = f32[64,2048]{1,0:T(8,128)} fusion(bf16[64,256]{1,0:T(8,128)(2,1)S(1)} %convert_element_type.80, bf16[256,2048]{1,0:T(8,128)(2,1)S(1)} %copy-done), kind=kOutput, calls=%fused_computation.100 | convolution fusion | flops 67108864 | bytes 1605632 | tf_op jit(solution)/shard_map/dot_general | solution.py:181
  48.9 0.0 reduce-scatter.2.cloned.1.call-update
  49.0 23.3 %reduce-scatter.2.cloned.1.call-done = f32[64,512]{1,0:T(8,128)} async-done(((f32[64,2048]{1,0:T(8,128)}), f32[64,512]{1,0:T(8,128)}) %reduce-scatter.2.cloned.1.call-update) | async-done | bytes 131088 | tf_op jit(solution)/shard_map/reduce_scatter | solution.py:182
  72.2 1.5 %convert_element_type.81 = bf16[64,512]{1,0:T(8,128)(2,1)} convert(f32[64,512]{1,0:T(8,128)} %reduce-scatter.2.cloned.1.call-done) | non-fusion elementwise | flops 32768 | bytes 196608 | tf_op jit(solution)/shard_map/convert_element_type | solution.py:182
  (21 shorter events, 0.2 us)
Async XLA Ops:
  6.5 41.3 %copy-start = (bf16[256,2048]{1,0:T(8,128)(2,1)S(1)}, bf16[256,2048]{1,0:T(8,128)(2,1)}, u32[]{:S(2)}) copy-start(bf16[256,2048]{1,0:T(8,128)(2,1)} %param.15) | copy-start | bytes 3145732
  6.5 22.7 %copy-start.1 = (bf16[64,2048]{1,0:T(8,128)(2,1)S(1)}, bf16[64,2048]{1,0:T(8,128)(2,1)}, u32[]{:S(2)}) copy-start(bf16[64,2048]{1,0:T(8,128)(2,1)} %param.11) | copy-start | bytes 786436
  6.5 22.0 %copy-start.4 = (s32[24]{0:T(128)S(1)}, s32[24]{0:T(128)}, u32[]{:S(2)}) copy-start(s32[24]{0:T(128)} %param.18) | copy-start | bytes 292
  6.5 21.8 %copy-start.5 = (s32[24]{0:T(128)S(1)}, s32[24]{0:T(128)}, u32[]{:S(2)}) copy-start(s32[24]{0:T(128)} %param.17) | copy-start | bytes 292
  6.5 22.7 %copy-start.2 = (bf16[2048,256]{1,0:T(8,128)(2,1)S(1)}, bf16[2048,256]{1,0:T(8,128)(2,1)}, u32[]{:S(2)}) copy-start(bf16[2048,256]{1,0:T(8,128)(2,1)} %param.12) | copy-start | bytes 3145732
  6.5 65.7 %reduce-scatter.2.cloned.1.call-start = ((), (), s32[]{:S(2)}) async-start(), calls=%async_computation.1 | async-start | bytes 655360 | tf_op jit(solution)/shard_map/reduce_scatter | solution.py:182
  13.6 16.8 %copy-start.3 = (bf16[1,3,64,128]{3,2,1,0:T(8,128)(2,1)S(1)}, bf16[1,3,64,128]{3,2,1,0:T(8,128)(2,1)}, u32[]{:S(2)}) copy-start(bf16[1,3,64,128]{3,2,1,0:T(8,128)(2,1)} %param.16) | copy-start | bytes 147460
  15.1 30.7 %collective-permute-start.3 = (bf16[64,1,128]{2,0,1:T(8,128)(2,1)S(1)}, bf16[64,1,128]{2,0,1:T(8,128)(2,1)S(1)}, u32[]{:S(2)}, u32[]{:S(2)}) collective-permute-start(bf16[64,1,128]{2,0,1:T(8,128)(2,1)S(1)} %pad_maximum_fusion.1), channel_id=1, source_target_pairs={{0,1},{1,2},{2,3},{3,4},{4,5},{5,6},{6,7},{8,9},{9,10},{10,11},{11... | collective-permute-start | bytes 49160 | tf_op jit(solution)/shard_map/ppermute | solution.py:20
  17.4 28.3 %collective-permute-start.2 = (bf16[64,1,128]{2,0,1:T(8,128)(2,1)S(1)}, bf16[64,1,128]{2,0,1:T(8,128)(2,1)S(1)}, u32[]{:S(2)}, u32[]{:S(2)}) collective-permute-start(bf16[64,1,128]{2,0,1:T(8,128)(2,1)S(1)} %pad_maximum_fusion.1), channel_id=1, source_target_pairs={{0,2},{1,3},{2,4},{3,5},{4,6},{5,7},{8,10},{9,11},{10,12},{11,13},... | collective-permute-start | bytes 49160 | tf_op jit(solution)/shard_map/ppermute | solution.py:20
  21.9 23.8 %collective-permute-start.1 = (bf16[64,1,128]{2,0,1:T(8,128)(2,1)S(1)}, bf16[64,1,128]{2,0,1:T(8,128)(2,1)S(1)}, u32[]{:S(2)}, u32[]{:S(2)}) collective-permute-start(bf16[64,1,128]{2,0,1:T(8,128)(2,1)S(1)} %pad_maximum_fusion.1), channel_id=1, source_target_pairs={{0,3},{1,4},{2,5},{3,6},{4,7},{8,11},{9,12},{10,13},{11,14},{12,15... | collective-permute-start | bytes 49160 | tf_op jit(solution)/shard_map/ppermute | solution.py:20
  26.4 19.3 %collective-permute-start = (bf16[64,1,128]{2,0,1:T(8,128)(2,1)S(1)}, bf16[64,1,128]{2,0,1:T(8,128)(2,1)S(1)}, u32[]{:S(2)}, u32[]{:S(2)}) collective-permute-start(bf16[64,1,128]{2,0,1:T(8,128)(2,1)S(1)} %pad_maximum_fusion.1), channel_id=1, source_target_pairs={{0,4},{1,5},{2,6},{3,7},{8,12},{9,13},{10,14},{11,15},{16,20},{17,... | collective-permute-start | bytes 49160 | tf_op jit(solution)/shard_map/ppermute | solution.py:20
Sparse Core Ops, SparseCore 0:
  49.1 23.0 reduce-scatter.1
where the time goes:
time: 81 us; the launch traced here: 80.6 us
  waiting for transfers between devices  23.3 us (29%)
  blocking collectives  14.6 us (18%)
  between operations  13.7 us (17%)
  starting transfers between devices  13.3 us (16%)
  other arithmetic  8.35 us (10%)
  matrix products  5.73 us (7%)
  local copies, waits for them, and re-layouts  1.67 us (2%)
    reduce_scatter x1, waiting for transfers between devices, local(): lax.psum_scatter(partial_out, 'head', scatter_dimension=1, tiled=True)  23.3 us
    all_gather x1, blocking collectives, local(): shard_pages = lax.all_gather(kv_pages, 'blk', axis=1, tiled=True)  14.6 us
    ppermute x4, starting transfers between devices, shifted(): lax.ppermute(value, axis, [(source, source + steps) for source in range(f...  13.3 us
  transfers between devices with their start and end apart: 5, of which 1 were waited for; matrix products, arithmetic and copies ran while one was open for 3% of the time, Pallas kernels for 0%

commit v1 on v0

v1 whole, which is shorter than its diff:
```python
import functools

import jax
import jax.numpy as jnp
import numpy as np
from jax import lax
from jax.experimental import pallas as pl
from jax.experimental.pallas import tpu as pltpu
from jax.sharding import PartitionSpec as P

HD = 64
MIDS = 8
GROUP = 8

NEGATIVE = -1e30
EPSILON = 1e-06
ROPE_BASE = 10000.0
SCORE_SCALE = 0.125
F32 = jnp.float32
VMEM_LIMIT = 48 * 1024 * 1024


def iota(shape, dim):
    return lax.broadcasted_iota(jnp.int32, shape, dim)


def as_column(row):
    count = row.shape[1]
    same = iota((count, count), 0) == iota((count, count), 1)
    return jnp.sum(jnp.where(same, row, 0.0), axis=1, keepdims=True)


def rotate(values, cosine, sine):
    low = (iota(values.shape, 1) % HD) < HD // 2
    partner = jnp.where(low, -pltpu.roll(values, 128 - HD // 2, 1), pltpu.roll(values, HD // 2, 1))
    return values * cosine + partner * sine


def keys_kernel(
    index_ref, freq_ref, tokens_ref, k_ref, v_ref, pages_ref, node_ref, fill_ref, len_ref, leaf_ref,
    parent_ref, own_ref, normed_ref, table_ref, meta_ref,
):
    rows = tokens_ref.shape[0]
    wide = tokens_ref[...].astype(F32)
    mean = jnp.mean(wide * wide, axis=-1, keepdims=True)
    normed = (wide * lax.rsqrt(mean + EPSILON)).astype(jnp.bfloat16)
    normed_ref[...] = normed

    node = as_column(node_ref[...].astype(F32))
    fill = as_column(fill_ref[...].astype(F32))
    length = len_ref[...].astype(F32)
    leaf = leaf_ref[...].astype(F32)
    parent = as_column(parent_ref[...].astype(F32))
    reqs, leaves = length.shape[1], parent.shape[0]
    before = iota((reqs, reqs), 0) < iota((reqs, reqs), 1)
    starts = jnp.sum(jnp.where(before, as_column(length), 0.0), axis=0, keepdims=True)
    ends = starts + length
    leaf_hit = iota((leaves, reqs), 0).astype(F32) == leaf
    mid_node = 1.0 + jnp.sum(jnp.where(leaf_hit, parent, 0.0), axis=0, keepdims=True)
    leaf_node = (1.0 + MIDS) + leaf
    on_path = (node == 0.0) | (node == mid_node) | (node == leaf_node)
    prefix = jnp.sum(jnp.where(on_path, fill, 0.0), axis=0, keepdims=True)
    place = (index_ref[0] * rows + iota((rows, 1), 0)).astype(F32)
    chosen = (place >= starts) & (place < ends)

    def of_row(values):
        return jnp.sum(jnp.where(chosen, values, 0.0), axis=1, keepdims=True)

    row_start, row_mid, row_leaf = of_row(starts), of_row(mid_node), of_row(leaf_node)
    position = of_row(prefix) + (place - row_start)
    for at, field in enumerate((row_start, row_mid, row_leaf)):
        meta_ref[at] = jnp.broadcast_to(field.astype(jnp.int32), (rows, 128))
    angles = position * freq_ref[...]
    cosine, sine = jnp.cos(angles), jnp.sin(angles)
    table_ref[0] = cosine
    table_ref[1] = sine

    keys = jnp.dot(normed, k_ref[...], preferred_element_type=F32)
    values = jnp.dot(normed, v_ref[...], preferred_element_type=F32)
    pack = jnp.concatenate([keys, values], axis=1)
    is_key = iota((rows, 128), 1) < HD
    pack = rotate(pack, jnp.where(is_key, cosine, 1.0), jnp.where(is_key, sine, 0.0))
    pages = pages_ref.shape[1]
    page_len = pages_ref.shape[2]
    for page in range(pages):
        own_ref[page * page_len : (page + 1) * page_len, :] = pages_ref[0, page]
    own_ref[pages * page_len :, :] = pack.astype(jnp.bfloat16)


def queries_kernel(
    pages, page_len, index_ref, ids_ref, node_ref, fill_ref, normed_ref, q_ref, table_ref, meta_ref,
    out_ref, bias_ref,
):
    rows = normed_ref.shape[0]
    heads = q_ref.shape[1] // HD
    cosine, sine = table_ref[0], table_ref[1]
    queries = jnp.dot(normed_ref[...], q_ref[...], preferred_element_type=F32)
    is_key = iota((rows, 128), 1) < HD
    for pair in range(heads // 2):
        turned = rotate(queries[:, pair * 128 : (pair + 1) * 128], cosine, sine)
        second = pltpu.roll(turned, HD, 1)
        for at, one in ((2 * pair, turned), (2 * pair + 1, second)):
            out_ref[at * rows : (at + 1) * rows, :] = jnp.where(is_key, one, 0.0).astype(jnp.bfloat16)
    place = index_ref[0] * rows + iota((rows, 128), 0)
    row_start, row_mid, row_leaf = meta_ref[0], meta_ref[1], meta_ref[2]
    lane = iota((rows, 128), 1)
    width = pages * page_len + rows

    def one_source(source, at):
        block = ids_ref[source]
        pieces = []
        for page in range(pages):
            number = block * pages + page
            slot = iota((rows, page_len), 1)
            node = node_ref[number]
            hit = (row_mid[:, :page_len] == node) | (row_leaf[:, :page_len] == node) | (node == 0)
            pieces.append(hit & (slot < fill_ref[number]))
        key_place = block * rows + iota((rows, rows), 1)
        pieces.append((key_place >= row_start[:, :rows]) & (key_place <= place[:, :rows]))
        bias = jnp.concatenate([jnp.where(ok, 0.0, NEGATIVE) for ok in pieces], axis=1)
        bias_ref[:, pl.ds(at, width)] = bias

    sources = ids_ref.shape[0]
    if sources <= GROUP:
        for source in range(sources):
            one_source(source, source * width)
    else:

        @pl.loop(0, sources)
        def _(source):
            one_source(source, pl.multiple_of(source * width, width))


def attend_kernel(steps, index_ref, q_ref, bias_ref, o_ref, *refs):
    *kv_refs, own_ref, out1_ref, out2_ref, out3_ref, top_ref, total_ref, accum_ref = refs
    rows = bias_ref.shape[0]
    heads = q_ref.shape[0] // rows
    keys = jnp.concatenate([ref[...] for ref in kv_refs], axis=0)
    scores = lax.dot_general(q_ref[...], keys, (((1,), (1,)), ((), ())), preferred_element_type=F32)
    count = keys.shape[0]
    scores = scores.reshape(heads, rows, count) * SCORE_SCALE + bias_ref[...][None]
    scores = scores.reshape(heads * rows, count)
    top = jnp.max(scores, axis=1, keepdims=True)

    def finish(accum, total):
        attended = accum / total
        second = pltpu.roll(attended, HD, 1)
        is_first = iota((rows, 128), 1) < HD
        parts = []
        for pair in range(heads // 2):
            first_head = second[2 * pair * rows : (2 * pair + 1) * rows]
            second_head = attended[(2 * pair + 1) * rows : (2 * pair + 2) * rows]
            parts.append(jnp.where(is_first, first_head, second_head))
        attended = jnp.concatenate(parts, axis=1).astype(jnp.bfloat16)
        columns = own_ref.shape[1]
        me = index_ref[1]
        for step, ref in enumerate((own_ref, out1_ref, out2_ref, out3_ref)):
            first = pl.multiple_of((me ^ step) * columns, columns)
            part = jnp.dot(attended, o_ref[:, pl.ds(first, columns)], preferred_element_type=F32)
            ref[...] = part.astype(ref.dtype)

    if steps == 1:
        weights = jnp.exp(scores - top)
        total = jnp.sum(weights, axis=1, keepdims=True)
        accum = jnp.dot(weights.astype(jnp.bfloat16), keys, preferred_element_type=F32)
        finish(accum, total)
        return

    step = pl.program_id(0)

    @pl.when(step == 0)
    def _():
        top_ref[...] = jnp.full(top_ref.shape, NEGATIVE, F32)
        total_ref[...] = jnp.zeros(total_ref.shape, F32)
        accum_ref[...] = jnp.zeros(accum_ref.shape, F32)

    top_old = top_ref[...][:, :1]
    top_new = jnp.maximum(top_old, top)
    weights = jnp.where(scores > 0.5 * NEGATIVE, jnp.exp(scores - top_new), 0.0)
    factor = jnp.exp(top_old - top_new)
    total = total_ref[...][:, :1] * factor + jnp.sum(weights, axis=1, keepdims=True)
    product = jnp.dot(weights.astype(jnp.bfloat16), keys, preferred_element_type=F32)
    accum = accum_ref[...] * factor + product
    top_ref[...] = jnp.broadcast_to(top_new, top_ref.shape)
    total_ref[...] = jnp.broadcast_to(total, total_ref.shape)
    accum_ref[...] = accum

    @pl.when(step == steps - 1)
    def _():
        finish(accum, total)


def smem():
    return pl.BlockSpec(memory_space=pltpu.SMEM)


def vmem():
    return pl.BlockSpec(memory_space=pltpu.VMEM)


def swapped(value, axis, distance):
    count = lax.axis_size(axis)
    return lax.ppermute(value, axis, [(device, device ^ distance) for device in range(count)])


def local(
    tokens, q_weight, k_weight, v_weight, o_weight, kv_pages, page_node, page_fill, req_len,
    req_leaf, leaf_parent,
):
    rows = tokens.shape[0]
    heads = q_weight.shape[1] // HD
    pages, page_len = kv_pages.shape[1:3]
    width = pages * page_len + rows
    columns = o_weight.shape[1] // 4
    blocks = lax.axis_size("blk")
    blk = lax.axis_index("blk")
    index = jnp.stack([blk, lax.axis_index("head")]).astype(jnp.int32)
    frequency = np.float64(ROPE_BASE) ** (-(np.arange(128) % (HD // 2)) / (HD // 2))
    frequency = jnp.asarray(frequency.astype(np.float32).reshape(1, 128))
    params = pltpu.CompilerParams(vmem_limit_bytes=VMEM_LIMIT)

    own, normed, table, meta = pl.pallas_call(
        keys_kernel,
        out_shape=(
            jax.ShapeDtypeStruct((width, 128), jnp.bfloat16),
            jax.ShapeDtypeStruct(tokens.shape, jnp.bfloat16),
            jax.ShapeDtypeStruct((2, rows, 128), F32),
            jax.ShapeDtypeStruct((3, rows, 128), jnp.int32),
        ),
        in_specs=[smem()] + [vmem()] * 10,
        out_specs=(vmem(),) * 4,
        compiler_params=params,
    )(
        index, frequency, tokens, k_weight, v_weight, kv_pages, page_node[None], page_fill[None],
        req_len[None], req_leaf[None], leaf_parent[None],
    )

    if blocks == GROUP:
        order = (0, 3, 5, 7, 1, 2, 4, 6)
        ids = blk ^ jnp.asarray(order, jnp.int32)
        crossed = [own] + [swapped(own, "blk", distance) for distance in order[1:4]]
        gathered = crossed + [swapped(value, "blk", 1) for value in crossed]
        steps = 1
    else:
        ids = jnp.arange(blocks, dtype=jnp.int32)
        gathered = [lax.all_gather(own, "blk", axis=0, tiled=True)]
        steps = blocks // GROUP

    queries, bias = pl.pallas_call(
        functools.partial(queries_kernel, pages, page_len),
        out_shape=(
            jax.ShapeDtypeStruct((heads * rows, 128), jnp.bfloat16),
            jax.ShapeDtypeStruct((rows, blocks * width), F32),
        ),
        in_specs=[smem()] * 4 + [vmem()] * 4,
        out_specs=(vmem(),) * 2,
        compiler_params=params,
        cost_estimate=pl.CostEstimate(flops=10**8, bytes_accessed=3 * 10**6, transcendentals=0),
    )(index, ids, page_node, page_fill, normed, q_weight, table, meta)

    part = jax.ShapeDtypeStruct((rows, columns), jnp.bfloat16)
    if steps == 1:
        kv_specs = [pl.BlockSpec((width, 128), lambda i: (0, 0))] * GROUP
    else:
        kv_specs = [pl.BlockSpec((GROUP * width, 128), lambda i: (i, 0))]
    whole = pl.BlockSpec((rows, columns), lambda i: (0, 0))
    sums = pl.pallas_call(
        functools.partial(attend_kernel, steps),
        grid=(steps,),
        out_shape=(jax.ShapeDtypeStruct((rows, columns), F32), part, part, part),
        in_specs=[
            smem(),
            pl.BlockSpec(queries.shape, lambda i: (0, 0)),
            pl.BlockSpec((rows, GROUP * width), lambda i: (0, i)),
            pl.BlockSpec(o_weight.shape, lambda i: (0, 0)),
        ]
        + kv_specs,
        out_specs=(whole,) * 4,
        scratch_shapes=[pltpu.VMEM((heads * rows, 128), F32)] * 3,
        compiler_params=params,
        cost_estimate=pl.CostEstimate(flops=10**9, bytes_accessed=3 * 10**6, transcendentals=10**6),
    )(index, queries, bias, o_weight, *gathered)
    total = sums[0]
    for distance in (1, 2, 3):
        total = total + swapped(sums[distance], "head", distance).astype(F32)
    return total.astype(jnp.bfloat16)


def solution(mesh):
    return jax.shard_map(
        local,
        mesh=mesh,
        in_specs=(
            P("blk", None), P(None, "head"), P(None, "head"), P(None, "head"), P("head", None),
            P("head", "blk", None, None), P(), P(), P(), P(), P(),
        ),
        out_specs=P("blk", "head"),
        check_vma=False,
    )
```

time: 81 us -> 26.6 us (0.33)
  blocking collectives: 14.6 us -> 0 us
  between operations: 13.7 us -> 0.19 us
  waiting for transfers between devices: 23.3 us -> 10.1 us
  other arithmetic: 8.35 us -> 0.74 us
  matrix products: 5.73 us -> 0 us
  Pallas kernels: 0 us -> 4.16 us
  starting transfers between devices: 13.3 us -> 9.71 us
    reduce_scatter x1 -> x0, waiting for transfers between devices: 23.3 us -> none  [local(): lax.psum_scatter(partial_out, 'head', scatter_dimension=1, tiled=True)]
    all_gather x1 -> x0, blocking collectives: 14.6 us -> none  [local(): shard_pages = lax.all_gather(kv_pages, 'blk', axis=1, tiled=True)]
    ppermute x4 -> x10, waiting for transfers between devices: 0.01 us -> 10.1 us  [swapped(): lax.ppermute(value, axis, [(device, device ^ distance) for device in rang...]
    dot_general x8 -> x0, matrix products: 5.73 us -> none  [the longest x1 1.32 us: local(): jnp.dot(normed, k_weight, preferred_element_type=jnp.float32)]
    reduce_sum x9 -> x0, other arithmetic: 4.3 us -> none  [the longest x1 1.1 us: norm_rows(): jnp.mean(wide * wide, axis=-1, keepdims=True) + EPSILON]
    pallas_call x0 -> x3, Pallas kernels: none -> 4.16 us  [the longest x1 1.98 us: local(): pl.pallas_call(functools.partial(attend_kernel, steps), grid=(steps,), ou...]
    ppermute x4 -> x10, starting transfers between devices: 13.3 us -> 9.71 us  [swapped(): lax.ppermute(value, axis, [(device, device ^ distance) for device in rang...]
    unnamed x16 -> x26, local copies, waits for them, and re-layouts: 0.06 us -> 1.6 us
  transfers between devices with their start and end apart: 5 -> 10, of which waited for: 1 -> 5; matrix products, arithmetic and copies ran while one was open for 3% -> 0% of each run, Pallas kernels for 0% -> 4%
where the time goes in v1:
time: 26.6 us; the launch traced here: 26.5 us
  waiting for transfers between devices  10.1 us (38%)
  starting transfers between devices  9.71 us (37%)
  Pallas kernels  4.16 us (16%)
  local copies, waits for them, and re-layouts  1.6 us (6%)
  other arithmetic  0.74 us (3%)
    ppermute x10, waiting for transfers between devices, swapped(): lax.ppermute(value, axis, [(device, device ^ distance) for device in rang...  10.1 us
    ppermute x10, starting transfers between devices, swapped(): lax.ppermute(value, axis, [(device, device ^ distance) for device in rang...  9.71 us
    pallas_call x1, Pallas kernels, local(): pl.pallas_call(functools.partial(attend_kernel, steps), grid=(steps,), ou...  1.98 us
    unnamed x26, local copies, waits for them, and re-layouts  1.6 us
    pallas_call x1, Pallas kernels, local(): pl.pallas_call(keys_kernel, out_shape=(jax.ShapeDtypeStruct((width, 128),...  1.13 us
    pallas_call x1, Pallas kernels, local(): pl.pallas_call(functools.partial(queries_kernel, pages, page_len), out_sh...  1.05 us
    convert_element_type x1, other arithmetic, local(): return total.astype(jnp.bfloat16)  0.66 us
  transfers between devices with their start and end apart: 10, of which 5 were waited for; matrix products, arithmetic and copies ran while one was open for 0% of the time, Pallas kernels for 4%

profile of v1, /device:TPU:0, one launch (start us, length us, event | category | flops | bytes accessed | tf_op | source)
XLA Modules:
  0.0 26.5 jit_solution(3718351967930107651)
XLA Ops:
  0.0 0.0 copy-start.10
  0.0 0.0 copy-start.1
  0.0 0.0 copy-start.2
  0.0 0.0 copy-start.3
  0.0 0.0 copy-start.4
  0.0 0.0 copy-start.5
  0.0 0.0 copy-start.6
  0.0 0.0 copy-start.7
  0.0 0.0 copy-start.8
  0.1 1.3 %copy.14.k_ref = bf16[2048,64]{1,0:T(8,128)(2,1)S(1)} copy(bf16[2048,64]{0,1:T(8,128)(2,1)} %param.15) | data formatting | bytes 524288 | tf_op args[2]
  1.3 0.0 copy-done.10
  1.3 0.0 copy-start
  1.4 0.3 %copy.15.v_ref = bf16[2048,64]{1,0:T(8,128)(2,1)S(1)} copy(bf16[2048,64]{0,1:T(8,128)(2,1)S(1)} %copy-done.10) | data formatting | bytes 524288 | tf_op args[3]
  1.6 0.1 pad_add_fusion.index_ref
  1.7 0.0 copy-done.1
  1.7 0.0 copy-done.2
  1.7 0.0 copy-done.3
  1.7 0.0 copy-done.4
  1.7 0.0 copy-done.5
  1.7 0.0 copy-done.6
  1.8 0.0 copy-done.7
  1.8 0.0 copy-done.8
  1.8 0.0 copy-start.11
  1.8 1.1 %shard_map.127 = (bf16[256,128]{1,0:T(8,128)(2,1)S(1)}, bf16[64,2048]{1,0:T(8,128)(2,1)S(1)}, f32[2,64,128]{2,1,0:T(8,128)S(1)}, s32[3,64,128]{2,1,0:T(8,128)S(1)}) custom-call(s32[2]{0:T(128)S(1)} %pad_add_fusion.index_ref, f32[1,128]{1,0:T(1,128)S(1)} %copy-done.8, bf16[64,2048]{1,0:T(8,128)(2,1)S(1)} %copy-done.1, bf16[2048,64]{1,0:T(8,128)(2,1)S(1)} %copy.14.k_ref, ...), custom_call_target="tpu_custom_call" | custom-call | tf_op jit(solution)/shard_map/pallas_call | solution.py:222
  2.9 0.0 copy-start.9
  2.9 4.6 %collective-permute-start.2 = (bf16[256,128]{1,0:T(8,128)(2,1)S(1)}, bf16[256,128]{1,0:T(8,128)(2,1)S(1)}, u32[]{:S(2)}, u32[]{:S(2)}) collective-permute-start(bf16[256,128]{1,0:T(8,128)(2,1)S(1)} %get-tuple-element.20.refs_0_), channel_id=1, source_target_pairs={{0,7},{1,6},{2,5},{3,4},{4,3},{5,2},{6,1},{7,0},{8,15},{9,14},{10,... | collective-permute-start | bytes 196616 | tf_op jit(solution)/shard_map/ppermute | solution.py:203
  7.5 0.0 collective-permute-start.1
  7.5 0.9 %collective-permute-start = (bf16[256,128]{1,0:T(8,128)(2,1)S(1)}, bf16[256,128]{1,0:T(8,128)(2,1)S(1)}, u32[]{:S(2)}, u32[]{:S(2)}) collective-permute-start(bf16[256,128]{1,0:T(8,128)(2,1)S(1)} %get-tuple-element.20.refs_0_), channel_id=1, source_target_pairs={{0,3},{1,2},{2,1},{3,0},{4,7},{5,6},{6,5},{7,4},{8,11},{9,10},{10,... | collective-permute-start | bytes 196616 | tf_op jit(solution)/shard_map/ppermute | solution.py:203
  8.4 0.0 collective-permute-start.3
  8.4 1.6 %collective-permute-done.2.refs_3_ = bf16[256,128]{1,0:T(8,128)(2,1)S(1)} collective-permute-done((bf16[256,128]{1,0:T(8,128)(2,1)S(1)}, bf16[256,128]{1,0:T(8,128)(2,1)S(1)}, u32[]{:S(2)}, u32[]{:S(2)}) %collective-permute-start.2) | collective-permute-done | bytes 65568 | tf_op jit(solution)/shard_map/ppermute | solution.py:203
  10.0 0.2 collective-permute-start.6
  10.2 3.8 %collective-permute-done.1.refs_2_ = bf16[256,128]{1,0:T(8,128)(2,1)S(1)} collective-permute-done((bf16[256,128]{1,0:T(8,128)(2,1)S(1)}, bf16[256,128]{1,0:T(8,128)(2,1)S(1)}, u32[]{:S(2)}, u32[]{:S(2)}) %collective-permute-start.1) | collective-permute-done | bytes 65568 | tf_op jit(solution)/shard_map/ppermute | solution.py:203
  13.9 0.1 collective-permute-start.5
  14.1 0.0 collective-permute-done.refs_1_
  14.1 0.4 %collective-permute-start.4 = (bf16[256,128]{1,0:T(8,128)(2,1)S(1)}, bf16[256,128]{1,0:T(8,128)(2,1)S(1)}, u32[]{:S(2)}, u32[]{:S(2)}) collective-permute-start(bf16[256,128]{1,0:T(8,128)(2,1)S(1)} %collective-permute-done.refs_1_), channel_id=1, source_target_pairs={{0,1},{1,0},{2,3},{3,2},{4,5},{5,4},{6,7},{7,6},{8,9},{9,8},{10,11... | collective-permute-start | bytes 196616 | tf_op jit(solution)/shard_map/ppermute | solution.py:203
  14.5 0.0 copy-done.11
  14.5 0.0 copy-done
  14.5 1.1 %shard_map.128 = (bf16[256,128]{1,0:T(8,128)(2,1)S(1)}, f32[64,2048]{1,0:T(8,128)S(1)}) custom-call(s32[2]{0:T(128)S(1)} %pad_add_fusion.index_ref, s32[8]{0:T(128)S(1)} %broadcast_xor_fusion.ids_ref, s32[24]{0:T(128)S(1)} %copy-done.3, s32[24]{0:T(128)S(1)} %copy-done.4, bf16[64,2048]{1,0:T(8,128)(2,1)S(1)} %get-tuple-element.15.normed_ref, ...), custom_call_target="tpu_custom_call" | custom-call | flops 100000000 | bytes 3000000 | tf_op jit(solution)/shard_map/pallas_call | solution.py:249
  15.5 0.0 collective-permute-done.3.refs_4_
  15.5 0.0 collective-permute-done.6.refs_7_
  15.5 0.0 collective-permute-done.5.refs_6_
  15.6 0.0 collective-permute-done.4.refs_5_
  15.6 0.0 copy-done.9
  15.6 2.0 %shard_map.129 = (f32[64,512]{1,0:T(8,128)S(1)}, bf16[64,512]{1,0:T(8,128)(2,1)S(1)}, bf16[64,512]{1,0:T(8,128)(2,1)S(1)}, bf16[64,512]{1,0:T(8,128)(2,1)S(1)}) custom-call(s32[2]{0:T(128)S(1)} %pad_add_fusion.index_ref, bf16[256,128]{1,0:T(8,128)(2,1)S(1)} %get-tuple-element.18.q_ref, f32[64,2048]{1,0:T(8,128)S(1)} %get-tuple-element.19.bias_ref, ...), custom_call_target="tpu_custom_call" | custom-call | flops 1000000000 | bytes 3000000 | tf_op jit(solution)/shard_map/pallas_call | solution.py:267
  17.6 1.6 %collective-permute-start.7 = (bf16[64,512]{1,0:T(8,128)(2,1)S(1)}, bf16[64,512]{1,0:T(8,128)(2,1)S(1)}, u32[]{:S(2)}, u32[]{:S(2)}) collective-permute-start(bf16[64,512]{1,0:T(8,128)(2,1)S(1)} %get-tuple-element.22), channel_id=1, source_target_pairs={{0,8},{8,0},{16,24},{24,16},{1,9},{9,1},{17,25},{25,17},{2,10},{10... | collective-permute-start | bytes 196616 | tf_op jit(solution)/shard_map/ppermute | solution.py:203
  19.1 1.5 %collective-permute-start.8 = (bf16[64,512]{1,0:T(8,128)(2,1)S(1)}, bf16[64,512]{1,0:T(8,128)(2,1)S(1)}, u32[]{:S(2)}, u32[]{:S(2)}) collective-permute-start(bf16[64,512]{1,0:T(8,128)(2,1)S(1)} %get-tuple-element.23), channel_id=1, source_target_pairs={{0,16},{8,24},{16,0},{24,8},{1,17},{9,25},{17,1},{25,9},{2,18},{10... | collective-permute-start | bytes 196616 | tf_op jit(solution)/shard_map/ppermute | solution.py:203
  20.6 0.5 %collective-permute-start.9 = (bf16[64,512]{1,0:T(8,128)(2,1)S(1)}, bf16[64,512]{1,0:T(8,128)(2,1)S(1)}, u32[]{:S(2)}, u32[]{:S(2)}) collective-permute-start(bf16[64,512]{1,0:T(8,128)(2,1)S(1)} %get-tuple-element.24), channel_id=1, source_target_pairs={{0,24},{8,16},{16,8},{24,0},{1,25},{9,17},{17,9},{25,1},{2,26},{10... | collective-permute-start | bytes 196616 | tf_op jit(solution)/shard_map/ppermute | solution.py:203
  21.1 0.8 %collective-permute-done.7 = bf16[64,512]{1,0:T(8,128)(2,1)S(1)} collective-permute-done((bf16[64,512]{1,0:T(8,128)(2,1)S(1)}, bf16[64,512]{1,0:T(8,128)(2,1)S(1)}, u32[]{:S(2)}, u32[]{:S(2)}) %collective-permute-start.7) | collective-permute-done | bytes 65568 | tf_op jit(solution)/shard_map/ppermute | solution.py:203
  21.9 1.5 %collective-permute-done.8 = bf16[64,512]{1,0:T(8,128)(2,1)S(1)} collective-permute-done((bf16[64,512]{1,0:T(8,128)(2,1)S(1)}, bf16[64,512]{1,0:T(8,128)(2,1)S(1)}, u32[]{:S(2)}, u32[]{:S(2)}) %collective-permute-start.8) | collective-permute-done | bytes 65568 | tf_op jit(solution)/shard_map/ppermute | solution.py:203
  23.4 2.4 %collective-permute-done.9 = bf16[64,512]{1,0:T(8,128)(2,1)S(1)} collective-permute-done((bf16[64,512]{1,0:T(8,128)(2,1)S(1)}, bf16[64,512]{1,0:T(8,128)(2,1)S(1)}, u32[]{:S(2)}, u32[]{:S(2)}) %collective-permute-start.9) | collective-permute-done | bytes 65568 | tf_op jit(solution)/shard_map/ppermute | solution.py:203
  25.8 0.7 %add_convert_fusion = bf16[64,512]{1,0:T(8,128)(2,1)} fusion(bf16[64,512]{1,0:T(8,128)(2,1)S(1)} %collective-permute-done.9, bf16[64,512]{1,0:T(8,128)(2,1)S(1)} %collective-permute-done.8, f32[64,512]{1,0:T(8,128)S(1)} %get-tuple-element.21, bf16[64,512]{1,0:T(8,128)(2,1)S(1)} %collective-permute-done.7), kind=kLoop, calls=%fused_computation | loop fusion | flops 229376 | bytes 393216 | tf_op jit(solution)/shard_map/convert_element_type | solution.py:286
  (1 shorter events, 0.0 us)
Async XLA Ops:
  0.0 1.3 %copy-start.10 = (bf16[2048,64]{0,1:T(8,128)(2,1)S(1)}, bf16[2048,64]{0,1:T(8,128)(2,1)}, u32[]{:S(2)}) copy-start(bf16[2048,64]{0,1:T(8,128)(2,1)} %param.16) | copy-start | bytes 786436
  0.0 1.7 %copy-start.1 = (bf16[64,2048]{1,0:T(8,128)(2,1)S(1)}, bf16[64,2048]{1,0:T(8,128)(2,1)}, u32[]{:S(2)}) copy-start(bf16[64,2048]{1,0:T(8,128)(2,1)} %tokens_ref.1) | copy-start | bytes 786436
  0.0 1.7 %copy-start.2 = (bf16[1,3,64,128]{3,2,1,0:T(8,128)(2,1)S(1)}, bf16[1,3,64,128]{3,2,1,0:T(8,128)(2,1)}, u32[]{:S(2)}) copy-start(bf16[1,3,64,128]{3,2,1,0:T(8,128)(2,1)} %pages_ref.1) | copy-start | bytes 147460
  0.0 1.7 %copy-start.3 = (s32[24]{0:T(128)S(1)}, s32[24]{0:T(128)}, u32[]{:S(2)}) copy-start(s32[24]{0:T(128)} %node_ref.1) | copy-start | bytes 292
  0.0 1.7 %copy-start.4 = (s32[24]{0:T(128)S(1)}, s32[24]{0:T(128)}, u32[]{:S(2)}) copy-start(s32[24]{0:T(128)} %fill_ref.1) | copy-start | bytes 292
  0.0 1.7 %copy-start.5 = (s32[4]{0:T(128)S(1)}, s32[4]{0:T(128)}, u32[]{:S(2)}) copy-start(s32[4]{0:T(128)} %param.21) | copy-start | bytes 52
  0.0 1.7 %copy-start.6 = (s32[4]{0:T(128)S(1)}, s32[4]{0:T(128)}, u32[]{:S(2)}) copy-start(s32[4]{0:T(128)} %param.22) | copy-start | bytes 52
  0.0 1.7 %copy-start.7 = (s32[4]{0:T(128)S(1)}, s32[4]{0:T(128)}, u32[]{:S(2)}) copy-start(s32[4]{0:T(128)} %param.23) | copy-start | bytes 52
  0.0 1.7 %copy-start.8 = (f32[1,128]{1,0:T(1,128)S(1)}, f32[1,128]{1,0:T(1,128)}, u32[]{:S(2)}) copy-start(f32[1,128]{1,0:T(1,128)} %constant.12.clone.freq_ref) | copy-start | bytes 1540
  1.3 13.1 %copy-start = (bf16[2048,256]{1,0:T(8,128)(2,1)S(1)}, bf16[2048,256]{1,0:T(8,128)(2,1)}, u32[]{:S(2)}) copy-start(bf16[2048,256]{1,0:T(8,128)(2,1)} %q_ref.1) | copy-start | bytes 3145732
  1.8 12.7 %copy-start.11 = (s32[8]{0:T(128)S(1)}, s32[8]{0:T(128)}, u32[]{:S(2)}) copy-start(s32[8]{0:T(128)} %constant.13.clone) | copy-start | bytes 100
  2.9 12.6 %copy-start.9 = (bf16[256,2048]{1,0:T(8,128)(2,1)S(1)}, bf16[256,2048]{1,0:T(8,128)(2,1)}, u32[]{:S(2)}) copy-start(bf16[256,2048]{1,0:T(8,128)(2,1)} %o_ref.1) | copy-start | bytes 3145732
  2.9 7.1 %collective-permute-start.2 = (bf16[256,128]{1,0:T(8,128)(2,1)S(1)}, bf16[256,128]{1,0:T(8,128)(2,1)S(1)}, u32[]{:S(2)}, u32[]{:S(2)}) collective-permute-start(bf16[256,128]{1,0:T(8,128)(2,1)S(1)} %get-tuple-element.20.refs_0_), channel_id=1, source_target_pairs={{0,7},{1,6},{2,5},{3,4},{4,3},{5,2},{6,1},{7,0},{8,15},{9,14},{10,... | collective-permute-start | bytes 196616 | tf_op jit(solution)/shard_map/ppermute | solution.py:203
  7.5 6.4 %collective-permute-start.1 = (bf16[256,128]{1,0:T(8,128)(2,1)S(1)}, bf16[256,128]{1,0:T(8,128)(2,1)S(1)}, u32[]{:S(2)}, u32[]{:S(2)}) collective-permute-start(bf16[256,128]{1,0:T(8,128)(2,1)S(1)} %get-tuple-element.20.refs_0_), channel_id=1, source_target_pairs={{0,5},{1,4},{2,7},{3,6},{4,1},{5,0},{6,3},{7,2},{8,13},{9,12},{10,... | collective-permute-start | bytes 196616 | tf_op jit(solution)/shard_map/ppermute | solution.py:203
  7.5 6.6 %collective-permute-start = (bf16[256,128]{1,0:T(8,128)(2,1)S(1)}, bf16[256,128]{1,0:T(8,128)(2,1)S(1)}, u32[]{:S(2)}, u32[]{:S(2)}) collective-permute-start(bf16[256,128]{1,0:T(8,128)(2,1)S(1)} %get-tuple-element.20.refs_0_), channel_id=1, source_target_pairs={{0,3},{1,2},{2,1},{3,0},{4,7},{5,6},{6,5},{7,4},{8,11},{9,10},{10,... | collective-permute-start | bytes 196616 | tf_op jit(solution)/shard_map/ppermute | solution.py:203
  8.4 7.1 %collective-permute-start.3 = (bf16[256,128]{1,0:T(8,128)(2,1)S(1)}, bf16[256,128]{1,0:T(8,128)(2,1)S(1)}, u32[]{:S(2)}, u32[]{:S(2)}) collective-permute-start(bf16[256,128]{1,0:T(8,128)(2,1)S(1)} %get-tuple-element.20.refs_0_), channel_id=1, source_target_pairs={{0,1},{1,0},{2,3},{3,2},{4,5},{5,4},{6,7},{7,6},{8,9},{9,8},{10,11... | collective-permute-start | bytes 196616 | tf_op jit(solution)/shard_map/ppermute | solution.py:203
  10.0 5.5 %collective-permute-start.6 = (bf16[256,128]{1,0:T(8,128)(2,1)S(1)}, bf16[256,128]{1,0:T(8,128)(2,1)S(1)}, u32[]{:S(2)}, u32[]{:S(2)}) collective-permute-start(bf16[256,128]{1,0:T(8,128)(2,1)S(1)} %collective-permute-done.2.refs_3_), channel_id=1, source_target_pairs={{0,1},{1,0},{2,3},{3,2},{4,5},{5,4},{6,7},{7,6},{8,9},{9,8},{10,11... | collective-permute-start | bytes 196616 | tf_op jit(solution)/shard_map/ppermute | solution.py:203
  13.9 1.6 %collective-permute-start.5 = (bf16[256,128]{1,0:T(8,128)(2,1)S(1)}, bf16[256,128]{1,0:T(8,128)(2,1)S(1)}, u32[]{:S(2)}, u32[]{:S(2)}) collective-permute-start(bf16[256,128]{1,0:T(8,128)(2,1)S(1)} %collective-permute-done.1.refs_2_), channel_id=1, source_target_pairs={{0,1},{1,0},{2,3},{3,2},{4,5},{5,4},{6,7},{7,6},{8,9},{9,8},{10,11... | collective-permute-start | bytes 196616 | tf_op jit(solution)/shard_map/ppermute | solution.py:203
  14.1 1.5 %collective-permute-start.4 = (bf16[256,128]{1,0:T(8,128)(2,1)S(1)}, bf16[256,128]{1,0:T(8,128)(2,1)S(1)}, u32[]{:S(2)}, u32[]{:S(2)}) collective-permute-start(bf16[256,128]{1,0:T(8,128)(2,1)S(1)} %collective-permute-done.refs_1_), channel_id=1, source_target_pairs={{0,1},{1,0},{2,3},{3,2},{4,5},{5,4},{6,7},{7,6},{8,9},{9,8},{10,11... | collective-permute-start | bytes 196616 | tf_op jit(solution)/shard_map/ppermute | solution.py:203
  17.6 4.3 %collective-permute-start.7 = (bf16[64,512]{1,0:T(8,128)(2,1)S(1)}, bf16[64,512]{1,0:T(8,128)(2,1)S(1)}, u32[]{:S(2)}, u32[]{:S(2)}) collective-permute-start(bf16[64,512]{1,0:T(8,128)(2,1)S(1)} %get-tuple-element.22), channel_id=1, source_target_pairs={{0,8},{8,0},{16,24},{24,16},{1,9},{9,1},{17,25},{25,17},{2,10},{10... | collective-permute-start | bytes 196616 | tf_op jit(solution)/shard_map/ppermute | solution.py:203
  19.1 4.3 %collective-permute-start.8 = (bf16[64,512]{1,0:T(8,128)(2,1)S(1)}, bf16[64,512]{1,0:T(8,128)(2,1)S(1)}, u32[]{:S(2)}, u32[]{:S(2)}) collective-permute-start(bf16[64,512]{1,0:T(8,128)(2,1)S(1)} %get-tuple-element.23), channel_id=1, source_target_pairs={{0,16},{8,24},{16,0},{24,8},{1,17},{9,25},{17,1},{25,9},{2,18},{10... | collective-permute-start | bytes 196616 | tf_op jit(solution)/shard_map/ppermute | solution.py:203
  20.6 5.2 %collective-permute-start.9 = (bf16[64,512]{1,0:T(8,128)(2,1)S(1)}, bf16[64,512]{1,0:T(8,128)(2,1)S(1)}, u32[]{:S(2)}, u32[]{:S(2)}) collective-permute-start(bf16[64,512]{1,0:T(8,128)(2,1)S(1)} %get-tuple-element.24), channel_id=1, source_target_pairs={{0,24},{8,16},{16,8},{24,0},{1,25},{9,17},{17,9},{25,1},{2,26},{10... | collective-permute-start | bytes 196616 | tf_op jit(solution)/shard_map/ppermute | solution.py:203

commit v2 on v1

v2 whole, which is shorter than its diff:
```python
import functools

import jax
import jax.numpy as jnp
import numpy as np
from jax import lax
from jax.experimental import pallas as pl
from jax.experimental.pallas import tpu as pltpu
from jax.sharding import PartitionSpec as P

HD = 64
MIDS = 8
GROUP = 8

NEGATIVE = -1e30
EPSILON = 1e-06
ROPE_BASE = 10000.0
SCORE_SCALE = 0.125
F32 = jnp.float32
BF16 = jnp.bfloat16
ROWS_BY_ROWS = (((1,), (1,)), ((), ()))
VMEM_LIMIT = 24 * 1024 * 1024


def iota(shape, dim):
    return lax.broadcasted_iota(jnp.int32, shape, dim)


def rotate(values, cosine, sine):
    low = (iota(values.shape, 1) % HD) < HD // 2
    partner = jnp.where(low, -pltpu.roll(values, 128 - HD // 2, 1), pltpu.roll(values, HD // 2, 1))
    return values * cosine + partner * sine


def fetch(sems, pairs):
    copies = [pltpu.make_async_copy(src, dst, sems.at[at]) for at, (src, dst) in enumerate(pairs)]
    for copy in copies:
        copy.start()
    return copies


def keys_kernel(
    freq_hbm, tokens_hbm, k_hbm, v_hbm, pages_hbm, node_hbm, fill_hbm, len_hbm, leaf_hbm,
    parent_hbm, own_ref, normed_ref, table_ref, meta_ref, tokens_ref, kv_ref, node_ref, fill_ref,
    len_ref, leaf_ref, parent_ref, freq_ref, held_ref, sems,
):
    rows = tokens_ref.shape[0]
    pages, page_len = pages_hbm.shape[1:3]
    small = (
        (node_hbm, node_ref), (fill_hbm, fill_ref), (len_hbm, len_ref), (leaf_hbm, leaf_ref),
        (parent_hbm, parent_ref), (freq_hbm, freq_ref),
    )
    large = (
        (tokens_hbm, tokens_ref),
        (k_hbm, kv_ref.at[pl.ds(0, HD)]),
        (v_hbm, kv_ref.at[pl.ds(HD, HD)]),
    )
    moved = tuple(
        (pages_hbm.at[0, page], own_ref.at[pl.ds(page * page_len, page_len)]) for page in range(pages)
    )
    copies = fetch(sems, small + large + moved)
    for copy in copies[: len(small)]:
        copy.wait()

    nodes = held_ref.shape[0]
    for node in range(nodes):
        held_ref[node] = 0

    def add_page(page, carry):
        node = node_ref[page]
        held_ref[node] = held_ref[node] + fill_ref[page]
        return carry

    lax.fori_loop(0, node_ref.shape[0], add_page, 0, unroll=node_ref.shape[0] <= 64)
    place = lax.axis_index("blk") * rows + iota((rows, 128), 0)

    def add_request(request, carry):
        start, row_start, row_mid, row_leaf, row_prefix = carry
        leaf = leaf_ref[request]
        mid_node = 1 + parent_ref[leaf]
        leaf_node = 1 + MIDS + leaf
        prefix = held_ref[0] + held_ref[mid_node] + held_ref[leaf_node]
        reached = place >= start
        return (
            start + len_ref[request],
            jnp.where(reached, start, row_start),
            jnp.where(reached, mid_node, row_mid),
            jnp.where(reached, leaf_node, row_leaf),
            jnp.where(reached, prefix, row_prefix),
        )

    zero = jnp.zeros((rows, 128), jnp.int32)
    reqs = len_ref.shape[0]
    _, row_start, row_mid, row_leaf, row_prefix = lax.fori_loop(
        0, reqs, add_request, (jnp.int32(0), zero, zero, zero, zero), unroll=reqs <= 8
    )
    meta_ref[0] = row_start
    meta_ref[1] = row_mid
    meta_ref[2] = row_leaf
    position = row_prefix + (place - row_start)
    angles = position.astype(F32) * freq_ref[...]
    cosine, sine = jnp.cos(angles), jnp.sin(angles)
    table_ref[0] = cosine
    table_ref[1] = sine

    copies[len(small)].wait()
    wide = tokens_ref[...].astype(F32)
    mean = jnp.mean(wide * wide, axis=-1, keepdims=True)
    normed = (wide * lax.rsqrt(mean + EPSILON)).astype(BF16)
    normed_ref[...] = normed
    copies[len(small) + 1].wait()
    copies[len(small) + 2].wait()
    pack = lax.dot_general(normed, kv_ref[...], ROWS_BY_ROWS, preferred_element_type=F32)
    is_key = iota((rows, 128), 1) < HD
    pack = rotate(pack, jnp.where(is_key, cosine, 1.0), jnp.where(is_key, sine, 0.0))
    own_ref[pages * page_len :, :] = pack.astype(BF16)
    for copy in copies[len(small) + 3 :]:
        copy.wait()


def queries_kernel(
    pages, page_len, order, normed_ref, table_ref, meta_ref, q_hbm, node_hbm, fill_hbm, out_ref,
    bias_ref, q_ref, node_ref, fill_ref, sems,
):
    copies = fetch(sems, ((node_hbm, node_ref), (fill_hbm, fill_ref), (q_hbm, q_ref)))
    rows = normed_ref.shape[0]
    heads = q_ref.shape[1] // HD
    me = lax.axis_index("blk")
    place = me * rows + iota((rows, 128), 0)
    row_start, row_mid, row_leaf = meta_ref[0], meta_ref[1], meta_ref[2]
    width = pages * page_len + rows
    sources = bias_ref.shape[1] // width
    copies[0].wait()
    copies[1].wait()

    def one_source(block, at):
        pieces = []
        for page in range(pages):
            number = block * pages + page
            slot = iota((rows, page_len), 1)
            node = node_ref[number]
            hit = (row_mid[:, :page_len] == node) | (row_leaf[:, :page_len] == node) | (node == 0)
            pieces.append(hit & (slot < fill_ref[number]))
        key_place = block * rows + iota((rows, rows), 1)
        pieces.append((key_place >= row_start[:, :rows]) & (key_place <= place[:, :rows]))
        bias = jnp.concatenate([jnp.where(ok, 0.0, NEGATIVE) for ok in pieces], axis=1)
        bias_ref[:, pl.ds(at, width)] = bias

    if order is not None:
        for source, flip in enumerate(order):
            one_source(me ^ flip, source * width)
    else:

        @pl.loop(0, sources)
        def _(source):
            one_source(source, pl.multiple_of(source * width, width))

    copies[2].wait()
    cosine, sine = table_ref[0], table_ref[1]
    queries = jnp.dot(normed_ref[...], q_ref[...], preferred_element_type=F32)
    is_key = iota((rows, 128), 1) < HD
    for pair in range(heads // 2):
        turned = rotate(queries[:, pair * 128 : (pair + 1) * 128], cosine, sine)
        second = pltpu.roll(turned, HD, 1)
        for at, one in ((2 * pair, turned), (2 * pair + 1, second)):
            out_ref[at * rows : (at + 1) * rows, :] = jnp.where(is_key, one, 0.0).astype(BF16)


def masked_scores(q_ref, bias_ref, keys):
    rows = bias_ref.shape[0]
    scores = lax.dot_general(q_ref[...], keys, ROWS_BY_ROWS, preferred_element_type=F32)
    heads, count = q_ref.shape[0] // rows, keys.shape[0]
    scores = scores.reshape(heads, rows, count) * SCORE_SCALE + bias_ref[...][None]
    return scores.reshape(heads * rows, count)


def fold(scores, keys, state):
    top = jnp.max(scores, axis=1, keepdims=True)
    if state is not None:
        top = jnp.maximum(state[0], top)
    weights = jnp.where(scores > 0.5 * NEGATIVE, jnp.exp(scores - top), 0.0)
    total = jnp.sum(weights, axis=1, keepdims=True)
    accum = jnp.dot(weights.astype(BF16), keys, preferred_element_type=F32)
    if state is not None:
        factor = jnp.exp(state[0] - top)
        total = total + state[1] * factor
        accum = accum + state[2] * factor
    return top, total, accum


def project(state, rows, o_ref, outs):
    _, total, accum = state
    attended = accum / total
    second = pltpu.roll(attended, HD, 1)
    is_first = iota((rows, 128), 1) < HD
    parts = []
    for pair in range(attended.shape[0] // rows // 2):
        first_head = second[2 * pair * rows : (2 * pair + 1) * rows]
        second_head = attended[(2 * pair + 1) * rows : (2 * pair + 2) * rows]
        parts.append(jnp.where(is_first, first_head, second_head))
    attended = jnp.concatenate(parts, axis=1).astype(BF16)
    columns = outs[0].shape[1]
    me = lax.axis_index("head")
    for step, ref in enumerate(outs):
        first = pl.multiple_of((me ^ step) * columns, columns)
        part = jnp.dot(attended, o_ref[:, pl.ds(first, columns)], preferred_element_type=F32)
        ref[...] = part.astype(ref.dtype)


def store_state(state, refs):
    for value, ref in zip(state, refs):
        ref[...] = jnp.broadcast_to(value, ref.shape)


def load_state(refs):
    top, total, accum = refs
    return top[...][:, :1], total[...][:, :1], accum[...]


def early_kernel(q_ref, bias_ref, *refs):
    *kv_refs, top_ref, total_ref, accum_ref = refs
    keys = jnp.concatenate([ref[...] for ref in kv_refs], axis=0)
    state = fold(masked_scores(q_ref, bias_ref, keys), keys, None)
    store_state(state, (top_ref, total_ref, accum_ref))


def late_kernel(sources, q_ref, bias_ref, o_hbm, *refs):
    kv_refs, state_refs, rest = refs[:sources], refs[sources : sources + 3], refs[sources + 3 :]
    *outs, o_ref, sems = rest
    copies = fetch(sems, ((o_hbm, o_ref),))
    keys = jnp.concatenate([ref[...] for ref in kv_refs], axis=0)
    state = fold(masked_scores(q_ref, bias_ref, keys), keys, load_state(state_refs))
    copies[0].wait()
    project(state, bias_ref.shape[0], o_ref, outs)


def looped_kernel(steps, q_ref, bias_ref, o_ref, kv_ref, *refs):
    *outs, top_ref, total_ref, accum_ref = refs
    state_refs = (top_ref, total_ref, accum_ref)
    step = pl.program_id(0)

    @pl.when(step == 0)
    def _():
        for ref, value in zip(state_refs, (NEGATIVE, 0.0, 0.0)):
            ref[...] = jnp.full(ref.shape, value, F32)

    keys = kv_ref[...]
    state = fold(masked_scores(q_ref, bias_ref, keys), keys, load_state(state_refs))
    store_state(state, state_refs)

    @pl.when(step == steps - 1)
    def _():
        project(load_state(state_refs), bias_ref.shape[0], o_ref, outs)


def vmem(count):
    return [pl.BlockSpec(memory_space=pltpu.VMEM)] * count


def hbm(count):
    return [pl.BlockSpec(memory_space=pltpu.HBM)] * count


def in_hbm(*values):
    return [pltpu.with_memory_space_constraint(value, pltpu.HBM) for value in values]


def shape(dims, kind=F32):
    return jax.ShapeDtypeStruct(dims, kind)


def swapped(value, axis, distance):
    count = lax.axis_size(axis)
    return lax.ppermute(value, axis, [(device, device ^ distance) for device in range(count)])


def cost(flops, moved):
    return pl.CostEstimate(flops=flops, bytes_accessed=moved, transcendentals=0)


def local(
    tokens, q_weight, k_weight, v_weight, o_weight, kv_pages, page_node, page_fill, req_len,
    req_leaf, leaf_parent,
):
    rows = tokens.shape[0]
    heads = q_weight.shape[1] // HD
    pages, page_len = kv_pages.shape[1:3]
    width = pages * page_len + rows
    shards = lax.axis_size("head")
    columns = o_weight.shape[1] // shards
    blocks = lax.axis_size("blk")
    ints = (page_node, page_fill, req_len, req_leaf, leaf_parent)
    frequency = np.float64(ROPE_BASE) ** (-(np.arange(128) % (HD // 2)) / (HD // 2))
    frequency = jnp.asarray(frequency.astype(np.float32).reshape(1, 128))
    params = pltpu.CompilerParams(vmem_limit_bytes=VMEM_LIMIT)

    own, normed, table, meta = pl.pallas_call(
        keys_kernel,
        out_shape=(
            shape((width, 128), BF16),
            shape(tokens.shape, BF16),
            shape((2, rows, 128)),
            shape((3, rows, 128), jnp.int32),
        ),
        in_specs=hbm(10),
        out_specs=tuple(vmem(4)),
        scratch_shapes=[pltpu.VMEM(tokens.shape, BF16), pltpu.VMEM((2 * HD, tokens.shape[1]), BF16)]
        + [pltpu.SMEM(value.shape, jnp.int32) for value in ints]
        + [
            pltpu.VMEM((1, 128), F32),
            pltpu.SMEM((1 + MIDS + leaf_parent.shape[0],), jnp.int32),
            pltpu.SemaphoreType.DMA((9 + pages,)),
        ],
        compiler_params=params,
    )(*in_hbm(frequency, tokens, k_weight.T, v_weight.T, kv_pages, *ints))

    small = blocks == GROUP
    order = (0, 1, 7, 6, 3, 2, 5, 4) if small else None
    queries, bias = pl.pallas_call(
        functools.partial(queries_kernel, pages, page_len, order),
        out_shape=(shape((heads * rows, 128), BF16), shape((rows, blocks * width))),
        in_specs=vmem(3) + hbm(3),
        out_specs=tuple(vmem(2)),
        scratch_shapes=[
            pltpu.VMEM(q_weight.shape, BF16),
            pltpu.SMEM(page_node.shape, jnp.int32),
            pltpu.SMEM(page_fill.shape, jnp.int32),
            pltpu.SemaphoreType.DMA((3,)),
        ],
        compiler_params=params,
        cost_estimate=cost(10**8, 3 * 10**6),
    )(normed, table, meta, *in_hbm(q_weight, page_node, page_fill))

    sums_shape = [shape((rows, columns))] + [shape((rows, columns), BF16)] * (shards - 1)
    state_shape = [shape((heads * rows, 128))] * 3
    if small:
        far, near, middle = (swapped(own, "blk", distance) for distance in (7, 3, 5))
        sibling = swapped(own, "blk", 1)
        far, queries = lax.optimization_barrier((far, queries))
        early = [own, sibling, far, swapped(far, "blk", 1), near, swapped(near, "blk", 1)]
        late = [middle, swapped(middle, "blk", 1)]
        cut = len(early) * width
        whole = [pl.BlockSpec(queries.shape, lambda i: (0, 0))]
        state = pl.pallas_call(
            early_kernel,
            grid=(1,),
            out_shape=state_shape,
            in_specs=whole
            + [pl.BlockSpec((rows, cut), lambda i: (0, 0))]
            + [pl.BlockSpec((width, 128), lambda i: (0, 0))] * len(early),
            out_specs=[pl.BlockSpec((heads * rows, 128), lambda i: (0, 0))] * 3,
            compiler_params=params,
            cost_estimate=cost(5 * 10**8, 3 * 10**6),
        )(queries, bias, *early)
        sums = pl.pallas_call(
            functools.partial(late_kernel, len(late)),
            grid=(1,),
            out_shape=sums_shape,
            in_specs=whole
            + [pl.BlockSpec((rows, blocks * width - cut), lambda i: (0, cut // (blocks * width - cut)))]
            + hbm(1)
            + [pl.BlockSpec((width, 128), lambda i: (0, 0))] * len(late)
            + [pl.BlockSpec((heads * rows, 128), lambda i: (0, 0))] * 3,
            out_specs=[pl.BlockSpec((rows, columns), lambda i: (0, 0))] * shards,
            scratch_shapes=[pltpu.VMEM(o_weight.shape, BF16), pltpu.SemaphoreType.DMA((1,))],
            compiler_params=params,
            cost_estimate=cost(5 * 10**8, 3 * 10**6),
        )(queries, bias, o_weight, *late, *state)
    else:
        gathered = lax.all_gather(own, "blk", axis=0, tiled=True)
        steps = blocks // GROUP
        sums = pl.pallas_call(
            functools.partial(looped_kernel, steps),
            grid=(steps,),
            out_shape=sums_shape,
            in_specs=[
                pl.BlockSpec(queries.shape, lambda i: (0, 0)),
                pl.BlockSpec((rows, GROUP * width), lambda i: (0, i)),
                pl.BlockSpec(o_weight.shape, lambda i: (0, 0)),
                pl.BlockSpec((GROUP * width, 128), lambda i: (i, 0)),
            ],
            out_specs=[pl.BlockSpec((rows, columns), lambda i: (0, 0))] * shards,
            scratch_shapes=[pltpu.VMEM((heads * rows, 128), F32)] * 3,
            compiler_params=params,
        )(queries, bias, o_weight, gathered)

    total = sums[0]
    for distance in range(1, shards):
        total = total + swapped(sums[distance], "head", distance).astype(F32)
    return total.astype(BF16)


def solution(mesh):
    return jax.shard_map(
        local,
        mesh=mesh,
        in_specs=(
            P("blk", None), P(None, "head"), P(None, "head"), P(None, "head"), P("head", None),
            P("head", "blk", None, None), P(), P(), P(), P(), P(),
        ),
        out_specs=P("blk", "head"),
        check_vma=False,
    )
```

time: 26.6 us -> 24.2 us (0.910)
  waiting for transfers between devices: 10.1 us -> 7.23 us
  local copies, waits for them, and re-layouts: 1.6 us -> 0.01 us
  Pallas kernels: 4.16 us -> 5.43 us
  starting transfers between devices: 9.71 us -> 10.6 us
    ppermute x10, waiting for transfers between devices: 10.1 us -> 7.23 us  [swapped(): lax.ppermute(value, axis, [(device, device ^ distance) for device in rang...]
    unnamed x26 -> x2, local copies, waits for them, and re-layouts: 1.6 us -> 0.01 us
    pallas_call x3 -> x4, Pallas kernels: 4.16 us -> 5.43 us  [the longest x1 1.71 us: local(): pl.pallas_call(functools.partial(queries_kernel, pages, page_len, order),...]
    ppermute x10, starting transfers between devices: 9.71 us -> 10.6 us  [swapped(): lax.ppermute(value, axis, [(device, device ^ distance) for device in rang...]
  transfers between devices with their start and end apart: 10 -> 10, of which waited for: 5 -> 5; matrix products, arithmetic and copies ran while one was open for 0% -> 0% of each run, Pallas kernels for 4% -> 11%
where the time goes in v2:
time: 24.2 us; the launch traced here: 24 us
  starting transfers between devices  10.6 us (44%)
  waiting for transfers between devices  7.23 us (30%)
  Pallas kernels  5.43 us (22%)
  other arithmetic  0.66 us (3%)
    ppermute x10, starting transfers between devices, swapped(): lax.ppermute(value, axis, [(device, device ^ distance) for device in rang...  10.6 us
    ppermute x10, waiting for transfers between devices, swapped(): lax.ppermute(value, axis, [(device, device ^ distance) for device in rang...  7.23 us
    pallas_call x1, Pallas kernels, local(): pl.pallas_call(functools.partial(queries_kernel, pages, page_len, order),...  1.71 us
    pallas_call x1, Pallas kernels, local(): pl.pallas_call(keys_kernel, out_shape=(shape((width, 128), BF16), shape(t...  1.61 us
    pallas_call x1, Pallas kernels, local(): pl.pallas_call(functools.partial(late_kernel, len(late)), grid=(1,), out_...  1.11 us
    pallas_call x1, Pallas kernels, local(): pl.pallas_call(early_kernel, grid=(1,), out_shape=state_shape, in_specs=w...  1 us
    convert_element_type x1, other arithmetic, local(): return total.astype(BF16)  0.66 us
  transfers between devices with their start and end apart: 10, of which 5 were waited for; matrix products, arithmetic and copies ran while one was open for 0% of the time, Pallas kernels for 11%

profile of v2, /device:TPU:0, one launch (start us, length us, event | category | flops | bytes accessed | tf_op | source)
XLA Modules:
  0.0 24.0 jit_solution(4689768539979473082)
XLA Ops:
  0.0 1.6 %shard_map.118 = (bf16[256,128]{1,0:T(8,128)(2,1)S(1)}, bf16[64,2048]{1,0:T(8,128)(2,1)S(1)}, f32[2,64,128]{2,1,0:T(8,128)S(1)}, s32[3,64,128]{2,1,0:T(8,128)S(1)}) custom-call(f32[1,128]{1,0:T(1,128)} %constant.2.clone.freq_hbm, bf16[64,2048]{1,0:T(8,128)(2,1)} %tokens_hbm.1, bf16[64,2048]{1,0:T(8,128)(2,1)} %bitcast.2, bf16[64,2048]{1,0:T(8,128)(2,1)} %bitcast.3, ...), custom_call_target="tpu_custom_call" | custom-call | tf_op jit(solution)/shard_map/pallas_call | solution.py:297
  1.6 4.6 %collective-permute-start = (bf16[256,128]{1,0:T(8,128)(2,1)S(1)}, bf16[256,128]{1,0:T(8,128)(2,1)S(1)}, u32[]{:S(2)}, u32[]{:S(2)}) collective-permute-start(bf16[256,128]{1,0:T(8,128)(2,1)S(1)} %get-tuple-element.20.refs_0_), channel_id=1, source_target_pairs={{0,7},{1,6},{2,5},{3,4},{4,3},{5,2},{6,1},{7,0},{8,15},{9,14},{10,... | collective-permute-start | bytes 196616 | tf_op jit(solution)/shard_map/ppermute | solution.py:274
  6.2 0.0 collective-permute-start.5
  6.2 0.9 %collective-permute-start.1 = (bf16[256,128]{1,0:T(8,128)(2,1)S(1)}, bf16[256,128]{1,0:T(8,128)(2,1)S(1)}, u32[]{:S(2)}, u32[]{:S(2)}) collective-permute-start(bf16[256,128]{1,0:T(8,128)(2,1)S(1)} %get-tuple-element.20.refs_0_), channel_id=1, source_target_pairs={{0,5},{1,4},{2,7},{3,6},{4,1},{5,0},{6,3},{7,2},{8,13},{9,12},{10,... | collective-permute-start | bytes 196616 | tf_op jit(solution)/shard_map/ppermute | solution.py:274
  7.1 0.0 collective-permute-start.3
  7.1 1.7 %shard_map.119 = (bf16[256,128]{1,0:T(8,128)(2,1)S(1)}, f32[64,2048]{1,0:T(8,128)S(1)}) custom-call(bf16[64,2048]{1,0:T(8,128)(2,1)S(1)} %get-tuple-element.21.normed_ref, f32[2,64,128]{2,1,0:T(8,128)S(1)} %get-tuple-element.22.table_ref, s32[3,64,128]{2,1,0:T(8,128)S(1)} %get-tuple-element.23.meta_ref, bf16[2048,256]{1,0:T(8,128)(2,1)} %q_hbm.1, ...), custom_call_target="tpu_custom_call" | custom-call | flops 100000000 | bytes 3000000 | tf_op jit(solution)/shard_map/pallas_call | solution.py:319
  8.8 0.0 copy-start
  8.8 0.0 collective-permute-done.refs_2_
  8.8 0.7 %collective-permute-start.4 = (bf16[256,128]{1,0:T(8,128)(2,1)S(1)}, bf16[256,128]{1,0:T(8,128)(2,1)S(1)}, u32[]{:S(2)}, u32[]{:S(2)}) collective-permute-start(bf16[256,128]{1,0:T(8,128)(2,1)S(1)} %collective-permute-done.refs_2_), channel_id=1, source_target_pairs={{0,1},{1,0},{2,3},{3,2},{4,5},{5,4},{6,7},{7,6},{8,9},{9,8},{10,11... | collective-permute-start | bytes 196616 | tf_op jit(solution)/shard_map/ppermute | solution.py:274
  9.6 1.6 %collective-permute-done.5.refs_4_ = bf16[256,128]{1,0:T(8,128)(2,1)S(1)} collective-permute-done((bf16[256,128]{1,0:T(8,128)(2,1)S(1)}, bf16[256,128]{1,0:T(8,128)(2,1)S(1)}, u32[]{:S(2)}, u32[]{:S(2)}) %collective-permute-start.5) | collective-permute-done | bytes 65568 | tf_op jit(solution)/shard_map/ppermute | solution.py:274
  11.2 0.9 %collective-permute-start.6 = (bf16[256,128]{1,0:T(8,128)(2,1)S(1)}, bf16[256,128]{1,0:T(8,128)(2,1)S(1)}, u32[]{:S(2)}, u32[]{:S(2)}) collective-permute-start(bf16[256,128]{1,0:T(8,128)(2,1)S(1)} %collective-permute-done.5.refs_4_), channel_id=1, source_target_pairs={{0,1},{1,0},{2,3},{3,2},{4,5},{5,4},{6,7},{7,6},{8,9},{9,8},{10,11... | collective-permute-start | bytes 196616 | tf_op jit(solution)/shard_map/ppermute | solution.py:274
  12.1 0.0 collective-permute-done.1.refs_0_
  12.1 0.0 collective-permute-start.2
  12.1 0.0 collective-permute-done.3.refs_1_
  12.1 0.0 collective-permute-done.4.refs_3_
  12.1 0.9 %collective-permute-done.6.refs_5_ = bf16[256,128]{1,0:T(8,128)(2,1)S(1)} collective-permute-done((bf16[256,128]{1,0:T(8,128)(2,1)S(1)}, bf16[256,128]{1,0:T(8,128)(2,1)S(1)}, u32[]{:S(2)}, u32[]{:S(2)}) %collective-permute-start.6) | collective-permute-done | bytes 65568 | tf_op jit(solution)/shard_map/ppermute | solution.py:274
  13.0 1.0 %shard_map.120 = (f32[256,128]{1,0:T(8,128)S(1)}, f32[256,128]{1,0:T(8,128)S(1)}, f32[256,128]{1,0:T(8,128)S(1)}) custom-call(bf16[256,128]{1,0:T(8,128)(2,1)S(1)} %get-tuple-element.25.q_ref, f32[64,2048]{1,0:T(8,128)S(1)} %get-tuple-element.26.bias_ref, bf16[256,128]{1,0:T(8,128)(2,1)S(1)} %get-tuple-element.20.refs_0_, ...), custom_call_target="tpu_custom_call" | custom-call | flops 500000000 | bytes 3000000 | tf_op jit(solution)/shard_map/pallas_call | solution.py:344
  14.0 0.0 collective-permute-done.2.refs_1_
  14.0 0.0 copy-done
  14.0 1.1 %shard_map.121 = (f32[64,512]{1,0:T(8,128)S(1)}, bf16[64,512]{1,0:T(8,128)(2,1)S(1)}, bf16[64,512]{1,0:T(8,128)(2,1)S(1)}, bf16[64,512]{1,0:T(8,128)(2,1)S(1)}) custom-call(bf16[256,128]{1,0:T(8,128)(2,1)S(1)} %get-tuple-element.25.q_ref, f32[64,2048]{1,0:T(8,128)S(1)} %get-tuple-element.26.bias_ref, bf16[256,2048]{1,0:T(8,128)(2,1)S(1)} %copy-done, ...), custom_call_target="tpu_custom_call" | custom-call | flops 500000000 | bytes 3000000 | tf_op jit(solution)/shard_map/pallas_call | solution.py:355
  15.1 1.6 %collective-permute-start.7 = (bf16[64,512]{1,0:T(8,128)(2,1)S(1)}, bf16[64,512]{1,0:T(8,128)(2,1)S(1)}, u32[]{:S(2)}, u32[]{:S(2)}) collective-permute-start(bf16[64,512]{1,0:T(8,128)(2,1)S(1)} %get-tuple-element.32), channel_id=1, source_target_pairs={{0,8},{8,0},{16,24},{24,16},{1,9},{9,1},{17,25},{25,17},{2,10},{10... | collective-permute-start | bytes 196616 | tf_op jit(solution)/shard_map/ppermute | solution.py:274
  16.7 1.5 %collective-permute-start.8 = (bf16[64,512]{1,0:T(8,128)(2,1)S(1)}, bf16[64,512]{1,0:T(8,128)(2,1)S(1)}, u32[]{:S(2)}, u32[]{:S(2)}) collective-permute-start(bf16[64,512]{1,0:T(8,128)(2,1)S(1)} %get-tuple-element.33), channel_id=1, source_target_pairs={{0,16},{8,24},{16,0},{24,8},{1,17},{9,25},{17,1},{25,9},{2,18},{10... | collective-permute-start | bytes 196616 | tf_op jit(solution)/shard_map/ppermute | solution.py:274
  18.2 0.5 %collective-permute-start.9 = (bf16[64,512]{1,0:T(8,128)(2,1)S(1)}, bf16[64,512]{1,0:T(8,128)(2,1)S(1)}, u32[]{:S(2)}, u32[]{:S(2)}) collective-permute-start(bf16[64,512]{1,0:T(8,128)(2,1)S(1)} %get-tuple-element.34), channel_id=1, source_target_pairs={{0,24},{8,16},{16,8},{24,0},{1,25},{9,17},{17,9},{25,1},{2,26},{10... | collective-permute-start | bytes 196616 | tf_op jit(solution)/shard_map/ppermute | solution.py:274
  18.7 0.9 %collective-permute-done.7 = bf16[64,512]{1,0:T(8,128)(2,1)S(1)} collective-permute-done((bf16[64,512]{1,0:T(8,128)(2,1)S(1)}, bf16[64,512]{1,0:T(8,128)(2,1)S(1)}, u32[]{:S(2)}, u32[]{:S(2)}) %collective-permute-start.7) | collective-permute-done | bytes 65568 | tf_op jit(solution)/shard_map/ppermute | solution.py:274
  19.5 1.4 %collective-permute-done.8 = bf16[64,512]{1,0:T(8,128)(2,1)S(1)} collective-permute-done((bf16[64,512]{1,0:T(8,128)(2,1)S(1)}, bf16[64,512]{1,0:T(8,128)(2,1)S(1)}, u32[]{:S(2)}, u32[]{:S(2)}) %collective-permute-start.8) | collective-permute-done | bytes 65568 | tf_op jit(solution)/shard_map/ppermute | solution.py:274
  20.9 2.4 %collective-permute-done.9 = bf16[64,512]{1,0:T(8,128)(2,1)S(1)} collective-permute-done((bf16[64,512]{1,0:T(8,128)(2,1)S(1)}, bf16[64,512]{1,0:T(8,128)(2,1)S(1)}, u32[]{:S(2)}, u32[]{:S(2)}) %collective-permute-start.9) | collective-permute-done | bytes 65568 | tf_op jit(solution)/shard_map/ppermute | solution.py:274
  23.4 0.7 %add_convert_fusion = bf16[64,512]{1,0:T(8,128)(2,1)} fusion(bf16[64,512]{1,0:T(8,128)(2,1)S(1)} %collective-permute-done.9, bf16[64,512]{1,0:T(8,128)(2,1)S(1)} %collective-permute-done.8, f32[64,512]{1,0:T(8,128)S(1)} %get-tuple-element.31, bf16[64,512]{1,0:T(8,128)(2,1)S(1)} %collective-permute-done.7), kind=kLoop, calls=%fused_computation | loop fusion | flops 229376 | bytes 393216 | tf_op jit(solution)/shard_map/convert_element_type | solution.py:390
Async XLA Ops:
  1.6 7.2 %collective-permute-start = (bf16[256,128]{1,0:T(8,128)(2,1)S(1)}, bf16[256,128]{1,0:T(8,128)(2,1)S(1)}, u32[]{:S(2)}, u32[]{:S(2)}) collective-permute-start(bf16[256,128]{1,0:T(8,128)(2,1)S(1)} %get-tuple-element.20.refs_0_), channel_id=1, source_target_pairs={{0,7},{1,6},{2,5},{3,4},{4,3},{5,2},{6,1},{7,0},{8,15},{9,14},{10,... | collective-permute-start | bytes 196616 | tf_op jit(solution)/shard_map/ppermute | solution.py:274
  6.2 5.0 %collective-permute-start.5 = (bf16[256,128]{1,0:T(8,128)(2,1)S(1)}, bf16[256,128]{1,0:T(8,128)(2,1)S(1)}, u32[]{:S(2)}, u32[]{:S(2)}) collective-permute-start(bf16[256,128]{1,0:T(8,128)(2,1)S(1)} %get-tuple-element.20.refs_0_), channel_id=1, source_target_pairs={{0,3},{1,2},{2,1},{3,0},{4,7},{5,6},{6,5},{7,4},{8,11},{9,10},{10,... | collective-permute-start | bytes 196616 | tf_op jit(solution)/shard_map/ppermute | solution.py:274
  6.2 5.9 %collective-permute-start.1 = (bf16[256,128]{1,0:T(8,128)(2,1)S(1)}, bf16[256,128]{1,0:T(8,128)(2,1)S(1)}, u32[]{:S(2)}, u32[]{:S(2)}) collective-permute-start(bf16[256,128]{1,0:T(8,128)(2,1)S(1)} %get-tuple-element.20.refs_0_), channel_id=1, source_target_pairs={{0,5},{1,4},{2,7},{3,6},{4,1},{5,0},{6,3},{7,2},{8,13},{9,12},{10,... | collective-permute-start | bytes 196616 | tf_op jit(solution)/shard_map/ppermute | solution.py:274
  7.1 5.0 %collective-permute-start.3 = (bf16[256,128]{1,0:T(8,128)(2,1)S(1)}, bf16[256,128]{1,0:T(8,128)(2,1)S(1)}, u32[]{:S(2)}, u32[]{:S(2)}) collective-permute-start(bf16[256,128]{1,0:T(8,128)(2,1)S(1)} %get-tuple-element.20.refs_0_), channel_id=1, source_target_pairs={{0,1},{1,0},{2,3},{3,2},{4,5},{5,4},{6,7},{7,6},{8,9},{9,8},{10,11... | collective-permute-start | bytes 196616 | tf_op jit(solution)/shard_map/ppermute | solution.py:274
  8.8 5.2 %copy-start = (bf16[256,2048]{1,0:T(8,128)(2,1)S(1)}, bf16[256,2048]{1,0:T(8,128)(2,1)}, u32[]{:S(2)}) copy-start(bf16[256,2048]{1,0:T(8,128)(2,1)} %o_hbm.1) | copy-start | bytes 3145732
  8.8 3.2 %collective-permute-start.4 = (bf16[256,128]{1,0:T(8,128)(2,1)S(1)}, bf16[256,128]{1,0:T(8,128)(2,1)S(1)}, u32[]{:S(2)}, u32[]{:S(2)}) collective-permute-start(bf16[256,128]{1,0:T(8,128)(2,1)S(1)} %collective-permute-done.refs_2_), channel_id=1, source_target_pairs={{0,1},{1,0},{2,3},{3,2},{4,5},{5,4},{6,7},{7,6},{8,9},{9,8},{10,11... | collective-permute-start | bytes 196616 | tf_op jit(solution)/shard_map/ppermute | solution.py:274
  11.2 1.8 %collective-permute-start.6 = (bf16[256,128]{1,0:T(8,128)(2,1)S(1)}, bf16[256,128]{1,0:T(8,128)(2,1)S(1)}, u32[]{:S(2)}, u32[]{:S(2)}) collective-permute-start(bf16[256,128]{1,0:T(8,128)(2,1)S(1)} %collective-permute-done.5.refs_4_), channel_id=1, source_target_pairs={{0,1},{1,0},{2,3},{3,2},{4,5},{5,4},{6,7},{7,6},{8,9},{9,8},{10,11... | collective-permute-start | bytes 196616 | tf_op jit(solution)/shard_map/ppermute | solution.py:274
  12.1 1.9 %collective-permute-start.2 = (bf16[256,128]{1,0:T(8,128)(2,1)S(1)}, bf16[256,128]{1,0:T(8,128)(2,1)S(1)}, u32[]{:S(2)}, u32[]{:S(2)}) collective-permute-start(bf16[256,128]{1,0:T(8,128)(2,1)S(1)} %collective-permute-done.1.refs_0_), channel_id=1, source_target_pairs={{0,1},{1,0},{2,3},{3,2},{4,5},{5,4},{6,7},{7,6},{8,9},{9,8},{10,11... | collective-permute-start | bytes 196616 | tf_op jit(solution)/shard_map/ppermute | solution.py:274
  15.1 4.4 %collective-permute-start.7 = (bf16[64,512]{1,0:T(8,128)(2,1)S(1)}, bf16[64,512]{1,0:T(8,128)(2,1)S(1)}, u32[]{:S(2)}, u32[]{:S(2)}) collective-permute-start(bf16[64,512]{1,0:T(8,128)(2,1)S(1)} %get-tuple-element.32), channel_id=1, source_target_pairs={{0,8},{8,0},{16,24},{24,16},{1,9},{9,1},{17,25},{25,17},{2,10},{10... | collective-permute-start | bytes 196616 | tf_op jit(solution)/shard_map/ppermute | solution.py:274
  16.7 4.3 %collective-permute-start.8 = (bf16[64,512]{1,0:T(8,128)(2,1)S(1)}, bf16[64,512]{1,0:T(8,128)(2,1)S(1)}, u32[]{:S(2)}, u32[]{:S(2)}) collective-permute-start(bf16[64,512]{1,0:T(8,128)(2,1)S(1)} %get-tuple-element.33), channel_id=1, source_target_pairs={{0,16},{8,24},{16,0},{24,8},{1,17},{9,25},{17,1},{25,9},{2,18},{10... | collective-permute-start | bytes 196616 | tf_op jit(solution)/shard_map/ppermute | solution.py:274
  18.2 5.2 %collective-permute-start.9 = (bf16[64,512]{1,0:T(8,128)(2,1)S(1)}, bf16[64,512]{1,0:T(8,128)(2,1)S(1)}, u32[]{:S(2)}, u32[]{:S(2)}) collective-permute-start(bf16[64,512]{1,0:T(8,128)(2,1)S(1)} %get-tuple-element.34), channel_id=1, source_target_pairs={{0,24},{8,16},{16,8},{24,0},{1,25},{9,17},{17,9},{25,1},{2,26},{10... | collective-permute-start | bytes 196616 | tf_op jit(solution)/shard_map/ppermute | solution.py:274

commit v3 on v2

--- a/solution.py
+++ b/solution.py
@@ -166,11 +166,11 @@
             out_ref[at * rows : (at + 1) * rows, :] = jnp.where(is_key, one, 0.0).astype(BF16)
 
 
-def masked_scores(q_ref, bias_ref, keys):
+def masked_scores(q_ref, bias_ref, keys, at=0):
     rows = bias_ref.shape[0]
     scores = lax.dot_general(q_ref[...], keys, ROWS_BY_ROWS, preferred_element_type=F32)
     heads, count = q_ref.shape[0] // rows, keys.shape[0]
-    scores = scores.reshape(heads, rows, count) * SCORE_SCALE + bias_ref[...][None]
+    scores = scores.reshape(heads, rows, count) * SCORE_SCALE + bias_ref[:, at : at + count][None]
     return scores.reshape(heads * rows, count)
 
 
@@ -217,19 +217,20 @@
     return top[...][:, :1], total[...][:, :1], accum[...]
 
 
-def early_kernel(q_ref, bias_ref, *refs):
-    *kv_refs, top_ref, total_ref, accum_ref = refs
+def early_kernel(sources, at, q_ref, bias_ref, *refs):
+    kv_refs, refs = refs[:sources], refs[sources:]
     keys = jnp.concatenate([ref[...] for ref in kv_refs], axis=0)
-    state = fold(masked_scores(q_ref, bias_ref, keys), keys, None)
-    store_state(state, (top_ref, total_ref, accum_ref))
-
-
-def late_kernel(sources, q_ref, bias_ref, o_hbm, *refs):
+    state = load_state(refs[:3]) if at else None
+    state = fold(masked_scores(q_ref, bias_ref, keys, at), keys, state)
+    store_state(state, refs[-3:])
+
+
+def late_kernel(sources, at, q_ref, bias_ref, o_hbm, *refs):
     kv_refs, state_refs, rest = refs[:sources], refs[sources : sources + 3], refs[sources + 3 :]
     *outs, o_ref, sems = rest
     copies = fetch(sems, ((o_hbm, o_ref),))
     keys = jnp.concatenate([ref[...] for ref in kv_refs], axis=0)
-    state = fold(masked_scores(q_ref, bias_ref, keys), keys, load_state(state_refs))
+    state = fold(masked_scores(q_ref, bias_ref, keys, at), keys, load_state(state_refs))
     copies[0].wait()
     project(state, bias_ref.shape[0], o_ref, outs)
 
@@ -315,7 +316,7 @@
     )(*in_hbm(frequency, tokens, k_weight.T, v_weight.T, kv_pages, *ints))
 
     small = blocks == GROUP
-    order = (0, 1, 7, 6, 3, 2, 5, 4) if small else None
+    order = (0, 7, 1, 6, 3, 5, 2, 4) if small else None
     queries, bias = pl.pallas_call(
         functools.partial(queries_kernel, pages, page_len, order),
         out_shape=(shape((heads * rows, 128), BF16), shape((rows, blocks * width))),
@@ -328,44 +329,39 @@
             pltpu.SemaphoreType.DMA((3,)),
         ],
         compiler_params=params,
-        cost_estimate=cost(10**8, 3 * 10**6),
+        cost_estimate=cost(1000, 1000),
     )(normed, table, meta, *in_hbm(q_weight, page_node, page_fill))
 
     sums_shape = [shape((rows, columns))] + [shape((rows, columns), BF16)] * (shards - 1)
     state_shape = [shape((heads * rows, 128))] * 3
     if small:
         far, near, middle = (swapped(own, "blk", distance) for distance in (7, 3, 5))
-        sibling = swapped(own, "blk", 1)
-        far, queries = lax.optimization_barrier((far, queries))
-        early = [own, sibling, far, swapped(far, "blk", 1), near, swapped(near, "blk", 1)]
-        late = [middle, swapped(middle, "blk", 1)]
-        cut = len(early) * width
-        whole = [pl.BlockSpec(queries.shape, lambda i: (0, 0))]
-        state = pl.pallas_call(
-            early_kernel,
-            grid=(1,),
-            out_shape=state_shape,
-            in_specs=whole
-            + [pl.BlockSpec((rows, cut), lambda i: (0, 0))]
-            + [pl.BlockSpec((width, 128), lambda i: (0, 0))] * len(early),
-            out_specs=[pl.BlockSpec((heads * rows, 128), lambda i: (0, 0))] * 3,
-            compiler_params=params,
-            cost_estimate=cost(5 * 10**8, 3 * 10**6),
-        )(queries, bias, *early)
+        far, again, queries = lax.optimization_barrier((far, own, queries))
+        first = [own, far]
+        second = [swapped(again, "blk", 1), swapped(far, "blk", 1), near, middle]
+        state = []
+        for sources, at in ((first, 0), (second, 2 * width)):
+            state = pl.pallas_call(
+                functools.partial(early_kernel, len(sources), at),
+                out_shape=state_shape,
+                in_specs=vmem(2 + len(sources) + len(state)),
+                out_specs=vmem(3),
+                compiler_params=params,
+                cost_estimate=cost(1000, 1000),
+            )(queries, bias, *sources, *state)
+            if at == 0:
+                near, *state = lax.optimization_barrier((near, *state))
+                second[2] = near
+        last = [swapped(near, "blk", 1), swapped(middle, "blk", 1)]
         sums = pl.pallas_call(
-            functools.partial(late_kernel, len(late)),
-            grid=(1,),
+            functools.partial(late_kernel, len(last), 6 * width),
             out_shape=sums_shape,
-            in_specs=whole
-            + [pl.BlockSpec((rows, blocks * width - cut), lambda i: (0, cut // (blocks * width - cut)))]
-            + hbm(1)
-            + [pl.BlockSpec((width, 128), lambda i: (0, 0))] * len(late)
-            + [pl.BlockSpec((heads * rows, 128), lambda i: (0, 0))] * 3,
-            out_specs=[pl.BlockSpec((rows, columns), lambda i: (0, 0))] * shards,
+            in_specs=vmem(2) + hbm(1) + vmem(len(last) + 3),
+            out_specs=vmem(shards),
             scratch_shapes=[pltpu.VMEM(o_weight.shape, BF16), pltpu.SemaphoreType.DMA((1,))],
             compiler_params=params,
-            cost_estimate=cost(5 * 10**8, 3 * 10**6),
-        )(queries, bias, o_weight, *late, *state)
+            cost_estimate=cost(1000, 1000),
+        )(queries, bias, o_weight, *last, *state)
     else:
         gathered = lax.all_gather(own, "blk", axis=0, tiled=True)
         steps = blocks // GROUP
@@ -385,7 +381,7 @@
         )(queries, bias, o_weight, gathered)
 
     total = sums[0]
-    for distance in range(1, shards):
+    for distance in (2, 3, 1):
         total = total + swapped(sums[distance], "head", distance).astype(F32)
     return total.astype(BF16)
 

time: 24.2 us -> 22.6 us (0.934)
  waiting for transfers between devices: 7.23 us -> 5.28 us
  Pallas kernels: 5.43 us -> 5.77 us
    ppermute x10, waiting for transfers between devices: 7.23 us -> 5.28 us  [swapped(): lax.ppermute(value, axis, [(device, device ^ distance) for device in rang...]
    pallas_call x2 -> x3, Pallas kernels: 2.11 us -> 2.45 us  [the longest x2 1.35 us: local(): pl.pallas_call(functools.partial(early_kernel, len(sources), at), out_sha...]
  transfers between devices with their start and end apart: 10 -> 10, of which waited for: 5 -> 4; matrix products, arithmetic and copies ran while one was open for 0% -> 0% of each run, Pallas kernels for 11% -> 14%
where the time goes in v3:
time: 22.6 us; the launch traced here: 22.4 us
  starting transfers between devices  10.6 us (47%)
  Pallas kernels  5.77 us (26%)
  waiting for transfers between devices  5.28 us (23%)
  other arithmetic  0.66 us (3%)
    ppermute x10, starting transfers between devices, swapped(): lax.ppermute(value, axis, [(device, device ^ distance) for device in rang...  10.6 us
    ppermute x10, waiting for transfers between devices, swapped(): lax.ppermute(value, axis, [(device, device ^ distance) for device in rang...  5.28 us
    pallas_call x1, Pallas kernels, local(): pl.pallas_call(functools.partial(queries_kernel, pages, page_len, order),...  1.71 us
    pallas_call x1, Pallas kernels, local(): pl.pallas_call(keys_kernel, out_shape=(shape((width, 128), BF16), shape(t...  1.61 us
    pallas_call x2, Pallas kernels, local(): pl.pallas_call(functools.partial(early_kernel, len(sources), at), out_sha...  1.35 us
    pallas_call x1, Pallas kernels, local(): pl.pallas_call(functools.partial(late_kernel, len(last), 6 * width), out_...  1.1 us
    convert_element_type x1, other arithmetic, local(): return total.astype(BF16)  0.66 us
  transfers between devices with their start and end apart: 10, of which 4 were waited for; matrix products, arithmetic and copies ran while one was open for 0% of the time, Pallas kernels for 14%

profile of v3, /device:TPU:0, one launch (start us, length us, event | category | flops | bytes accessed | tf_op | source)
XLA Modules:
  0.0 22.4 jit_solution(12482771738828261992)
XLA Ops:
  0.0 1.6 %shard_map.118 = (bf16[256,128]{1,0:T(8,128)(2,1)S(1)}, bf16[64,2048]{1,0:T(8,128)(2,1)S(1)}, f32[2,64,128]{2,1,0:T(8,128)S(1)}, s32[3,64,128]{2,1,0:T(8,128)S(1)}) custom-call(f32[1,128]{1,0:T(1,128)} %constant.2.clone.freq_hbm, bf16[64,2048]{1,0:T(8,128)(2,1)} %tokens_hbm.1, bf16[64,2048]{1,0:T(8,128)(2,1)} %bitcast.2, bf16[64,2048]{1,0:T(8,128)(2,1)} %bitcast.3, ...), custom_call_target="tpu_custom_call" | custom-call | tf_op jit(solution)/shard_map/pallas_call | solution.py:298
  1.6 4.6 %collective-permute-start = (bf16[256,128]{1,0:T(8,128)(2,1)S(1)}, bf16[256,128]{1,0:T(8,128)(2,1)S(1)}, u32[]{:S(2)}, u32[]{:S(2)}) collective-permute-start(bf16[256,128]{1,0:T(8,128)(2,1)S(1)} %get-tuple-element.40.refs_0_), channel_id=1, source_target_pairs={{0,7},{1,6},{2,5},{3,4},{4,3},{5,2},{6,1},{7,0},{8,15},{9,14},{10,... | collective-permute-start | bytes 196616 | tf_op jit(solution)/shard_map/ppermute | solution.py:275
  6.2 0.0 collective-permute-start.1
  6.2 0.9 %collective-permute-start.3 = (bf16[256,128]{1,0:T(8,128)(2,1)S(1)}, bf16[256,128]{1,0:T(8,128)(2,1)S(1)}, u32[]{:S(2)}, u32[]{:S(2)}) collective-permute-start(bf16[256,128]{1,0:T(8,128)(2,1)S(1)} %get-tuple-element.40.refs_0_), channel_id=1, source_target_pairs={{0,5},{1,4},{2,7},{3,6},{4,1},{5,0},{6,3},{7,2},{8,13},{9,12},{10,... | collective-permute-start | bytes 196616 | tf_op jit(solution)/shard_map/ppermute | solution.py:275
  7.1 1.7 %shard_map.119 = (bf16[256,128]{1,0:T(8,128)(2,1)S(1)}, f32[64,2048]{1,0:T(8,128)S(1)}) custom-call(bf16[64,2048]{1,0:T(8,128)(2,1)S(1)} %get-tuple-element.29.normed_ref, f32[2,64,128]{2,1,0:T(8,128)S(1)} %get-tuple-element.30.table_ref, s32[3,64,128]{2,1,0:T(8,128)S(1)} %get-tuple-element.31.meta_ref, bf16[2048,256]{1,0:T(8,128)(2,1)} %q_hbm.1, ...), custom_call_target="tpu_custom_call" | custom-call | flops 1000 | bytes 1000 | tf_op jit(solution)/shard_map/pallas_call | solution.py:320
  8.8 0.0 copy-start
  8.8 0.0 collective-permute-done.refs_1_
  8.8 0.7 %collective-permute-start.6 = (bf16[256,128]{1,0:T(8,128)(2,1)S(1)}, bf16[256,128]{1,0:T(8,128)(2,1)S(1)}, u32[]{:S(2)}, u32[]{:S(2)}) collective-permute-start(bf16[256,128]{1,0:T(8,128)(2,1)S(1)} %collective-permute-done.refs_1_), channel_id=1, source_target_pairs={{0,1},{1,0},{2,3},{3,2},{4,5},{5,4},{6,7},{7,6},{8,9},{9,8},{10,11... | collective-permute-start | bytes 196616 | tf_op jit(solution)/shard_map/ppermute | solution.py:275
  9.6 0.0 collective-permute-start.5
  9.6 0.5 %shard_map.120 = (f32[256,128]{1,0:T(8,128)S(1)}, f32[256,128]{1,0:T(8,128)S(1)}, f32[256,128]{1,0:T(8,128)S(1)}) custom-call(bf16[256,128]{1,0:T(8,128)(2,1)S(1)} %get-tuple-element.33.q_ref, f32[64,2048]{1,0:T(8,128)S(1)} %get-tuple-element.34.bias_ref, bf16[256,128]{1,0:T(8,128)(2,1)S(1)} %get-tuple-element.40.refs_0_, ...), custom_call_target="tpu_custom_call" | custom-call | flops 1000 | bytes 1000 | tf_op jit(solution)/shard_map/pallas_call | solution.py:344
  10.0 1.2 %collective-permute-done.1.refs_2_ = bf16[256,128]{1,0:T(8,128)(2,1)S(1)} collective-permute-done((bf16[256,128]{1,0:T(8,128)(2,1)S(1)}, bf16[256,128]{1,0:T(8,128)(2,1)S(1)}, u32[]{:S(2)}, u32[]{:S(2)}) %collective-permute-start.1) | collective-permute-done | bytes 65568 | tf_op jit(solution)/shard_map/ppermute | solution.py:275
  11.2 0.9 %collective-permute-start.2 = (bf16[256,128]{1,0:T(8,128)(2,1)S(1)}, bf16[256,128]{1,0:T(8,128)(2,1)S(1)}, u32[]{:S(2)}, u32[]{:S(2)}) collective-permute-start(bf16[256,128]{1,0:T(8,128)(2,1)S(1)} %collective-permute-done.1.refs_2_), channel_id=1, source_target_pairs={{0,1},{1,0},{2,3},{3,2},{4,5},{5,4},{6,7},{7,6},{8,9},{9,8},{10,11... | collective-permute-start | bytes 196616 | tf_op jit(solution)/shard_map/ppermute | solution.py:275
  12.1 0.0 collective-permute-done.3.refs_3_
  12.1 0.0 collective-permute-start.4
  12.1 0.0 collective-permute-done.6.refs_1_
  12.1 0.0 collective-permute-done.5.refs_0_
  12.1 0.9 %shard_map.121 = (f32[256,128]{1,0:T(8,128)S(1)}, f32[256,128]{1,0:T(8,128)S(1)}, f32[256,128]{1,0:T(8,128)S(1)}) custom-call(bf16[256,128]{1,0:T(8,128)(2,1)S(1)} %get-tuple-element.33.q_ref, f32[64,2048]{1,0:T(8,128)S(1)} %get-tuple-element.34.bias_ref, bf16[256,128]{1,0:T(8,128)(2,1)S(1)} %collective-permute-done.5.refs_0_, ...), custom_call_target="tpu_custom_call" | custom-call | flops 1000 | bytes 1000 | tf_op jit(solution)/shard_map/pallas_call | solution.py:344
  13.0 0.0 collective-permute-done.2.refs_0_
  13.0 0.3 %collective-permute-done.4.refs_1_ = bf16[256,128]{1,0:T(8,128)(2,1)S(1)} collective-permute-done((bf16[256,128]{1,0:T(8,128)(2,1)S(1)}, bf16[256,128]{1,0:T(8,128)(2,1)S(1)}, u32[]{:S(2)}, u32[]{:S(2)}) %collective-permute-start.4) | collective-permute-done | bytes 65568 | tf_op jit(solution)/shard_map/ppermute | solution.py:275
  13.3 0.0 copy-done
  13.3 1.1 %shard_map.122 = (f32[64,512]{1,0:T(8,128)S(1)}, bf16[64,512]{1,0:T(8,128)(2,1)S(1)}, bf16[64,512]{1,0:T(8,128)(2,1)S(1)}, bf16[64,512]{1,0:T(8,128)(2,1)S(1)}) custom-call(bf16[256,128]{1,0:T(8,128)(2,1)S(1)} %get-tuple-element.33.q_ref, f32[64,2048]{1,0:T(8,128)S(1)} %get-tuple-element.34.bias_ref, bf16[256,2048]{1,0:T(8,128)(2,1)S(1)} %copy-done, ...), custom_call_target="tpu_custom_call" | custom-call | flops 1000 | bytes 1000 | tf_op jit(solution)/shard_map/pallas_call | solution.py:356
  14.4 1.6 %collective-permute-start.7 = (bf16[64,512]{1,0:T(8,128)(2,1)S(1)}, bf16[64,512]{1,0:T(8,128)(2,1)S(1)}, u32[]{:S(2)}, u32[]{:S(2)}) collective-permute-start(bf16[64,512]{1,0:T(8,128)(2,1)S(1)} %get-tuple-element.48), channel_id=1, source_target_pairs={{0,16},{8,24},{16,0},{24,8},{1,17},{9,25},{17,1},{25,9},{2,18},{10... | collective-permute-start | bytes 196616 | tf_op jit(solution)/shard_map/ppermute | solution.py:275
  16.0 1.4 %collective-permute-start.8 = (bf16[64,512]{1,0:T(8,128)(2,1)S(1)}, bf16[64,512]{1,0:T(8,128)(2,1)S(1)}, u32[]{:S(2)}, u32[]{:S(2)}) collective-permute-start(bf16[64,512]{1,0:T(8,128)(2,1)S(1)} %get-tuple-element.49), channel_id=1, source_target_pairs={{0,24},{8,16},{16,8},{24,0},{1,25},{9,17},{17,9},{25,1},{2,26},{10... | collective-permute-start | bytes 196616 | tf_op jit(solution)/shard_map/ppermute | solution.py:275
  17.4 0.5 %collective-permute-start.9 = (bf16[64,512]{1,0:T(8,128)(2,1)S(1)}, bf16[64,512]{1,0:T(8,128)(2,1)S(1)}, u32[]{:S(2)}, u32[]{:S(2)}) collective-permute-start(bf16[64,512]{1,0:T(8,128)(2,1)S(1)} %get-tuple-element.50), channel_id=1, source_target_pairs={{0,8},{8,0},{16,24},{24,16},{1,9},{9,1},{17,25},{25,17},{2,10},{10... | collective-permute-start | bytes 196616 | tf_op jit(solution)/shard_map/ppermute | solution.py:275
  18.0 0.8 %collective-permute-done.7 = bf16[64,512]{1,0:T(8,128)(2,1)S(1)} collective-permute-done((bf16[64,512]{1,0:T(8,128)(2,1)S(1)}, bf16[64,512]{1,0:T(8,128)(2,1)S(1)}, u32[]{:S(2)}, u32[]{:S(2)}) %collective-permute-start.7) | collective-permute-done | bytes 65568 | tf_op jit(solution)/shard_map/ppermute | solution.py:275
  18.7 3.0 %collective-permute-done.8 = bf16[64,512]{1,0:T(8,128)(2,1)S(1)} collective-permute-done((bf16[64,512]{1,0:T(8,128)(2,1)S(1)}, bf16[64,512]{1,0:T(8,128)(2,1)S(1)}, u32[]{:S(2)}, u32[]{:S(2)}) %collective-permute-start.8) | collective-permute-done | bytes 65568 | tf_op jit(solution)/shard_map/ppermute | solution.py:275
  21.7 0.0 collective-permute-done.9
  21.7 0.7 %add_convert_fusion = bf16[64,512]{1,0:T(8,128)(2,1)} fusion(bf16[64,512]{1,0:T(8,128)(2,1)S(1)} %collective-permute-done.9, bf16[64,512]{1,0:T(8,128)(2,1)S(1)} %collective-permute-done.8, f32[64,512]{1,0:T(8,128)S(1)} %get-tuple-element.47, bf16[64,512]{1,0:T(8,128)(2,1)S(1)} %collective-permute-done.7), kind=kLoop, calls=%fused_computation | loop fusion | flops 229376 | bytes 393216 | tf_op jit(solution)/shard_map/convert_element_type | solution.py:386
Async XLA Ops:
  1.6 7.2 %collective-permute-start = (bf16[256,128]{1,0:T(8,128)(2,1)S(1)}, bf16[256,128]{1,0:T(8,128)(2,1)S(1)}, u32[]{:S(2)}, u32[]{:S(2)}) collective-permute-start(bf16[256,128]{1,0:T(8,128)(2,1)S(1)} %get-tuple-element.40.refs_0_), channel_id=1, source_target_pairs={{0,7},{1,6},{2,5},{3,4},{4,3},{5,2},{6,1},{7,0},{8,15},{9,14},{10,... | collective-permute-start | bytes 196616 | tf_op jit(solution)/shard_map/ppermute | solution.py:275
  6.2 5.0 %collective-permute-start.1 = (bf16[256,128]{1,0:T(8,128)(2,1)S(1)}, bf16[256,128]{1,0:T(8,128)(2,1)S(1)}, u32[]{:S(2)}, u32[]{:S(2)}) collective-permute-start(bf16[256,128]{1,0:T(8,128)(2,1)S(1)} %get-tuple-element.40.refs_0_), channel_id=1, source_target_pairs={{0,3},{1,2},{2,1},{3,0},{4,7},{5,6},{6,5},{7,4},{8,11},{9,10},{10,... | collective-permute-start | bytes 196616 | tf_op jit(solution)/shard_map/ppermute | solution.py:275
  6.2 5.9 %collective-permute-start.3 = (bf16[256,128]{1,0:T(8,128)(2,1)S(1)}, bf16[256,128]{1,0:T(8,128)(2,1)S(1)}, u32[]{:S(2)}, u32[]{:S(2)}) collective-permute-start(bf16[256,128]{1,0:T(8,128)(2,1)S(1)} %get-tuple-element.40.refs_0_), channel_id=1, source_target_pairs={{0,5},{1,4},{2,7},{3,6},{4,1},{5,0},{6,3},{7,2},{8,13},{9,12},{10,... | collective-permute-start | bytes 196616 | tf_op jit(solution)/shard_map/ppermute | solution.py:275
  8.8 4.5 %copy-start = (bf16[256,2048]{1,0:T(8,128)(2,1)S(1)}, bf16[256,2048]{1,0:T(8,128)(2,1)}, u32[]{:S(2)}) copy-start(bf16[256,2048]{1,0:T(8,128)(2,1)} %o_hbm.1) | copy-start | bytes 3145732
  8.8 3.2 %collective-permute-start.6 = (bf16[256,128]{1,0:T(8,128)(2,1)S(1)}, bf16[256,128]{1,0:T(8,128)(2,1)S(1)}, u32[]{:S(2)}, u32[]{:S(2)}) collective-permute-start(bf16[256,128]{1,0:T(8,128)(2,1)S(1)} %collective-permute-done.refs_1_), channel_id=1, source_target_pairs={{0,1},{1,0},{2,3},{3,2},{4,5},{5,4},{6,7},{7,6},{8,9},{9,8},{10,11... | collective-permute-start | bytes 196616 | tf_op jit(solution)/shard_map/ppermute | solution.py:275
  9.6 2.5 %collective-permute-start.5 = (bf16[256,128]{1,0:T(8,128)(2,1)S(1)}, bf16[256,128]{1,0:T(8,128)(2,1)S(1)}, u32[]{:S(2)}, u32[]{:S(2)}) collective-permute-start(bf16[256,128]{1,0:T(8,128)(2,1)S(1)} %get-tuple-element.40.refs_0_), channel_id=1, source_target_pairs={{0,1},{1,0},{2,3},{3,2},{4,5},{5,4},{6,7},{7,6},{8,9},{9,8},{10,11... | collective-permute-start | bytes 196616 | tf_op jit(solution)/shard_map/ppermute | solution.py:275
  11.2 1.8 %collective-permute-start.2 = (bf16[256,128]{1,0:T(8,128)(2,1)S(1)}, bf16[256,128]{1,0:T(8,128)(2,1)S(1)}, u32[]{:S(2)}, u32[]{:S(2)}) collective-permute-start(bf16[256,128]{1,0:T(8,128)(2,1)S(1)} %collective-permute-done.1.refs_2_), channel_id=1, source_target_pairs={{0,1},{1,0},{2,3},{3,2},{4,5},{5,4},{6,7},{7,6},{8,9},{9,8},{10,11... | collective-permute-start | bytes 196616 | tf_op jit(solution)/shard_map/ppermute | solution.py:275
  12.1 1.3 %collective-permute-start.4 = (bf16[256,128]{1,0:T(8,128)(2,1)S(1)}, bf16[256,128]{1,0:T(8,128)(2,1)S(1)}, u32[]{:S(2)}, u32[]{:S(2)}) collective-permute-start(bf16[256,128]{1,0:T(8,128)(2,1)S(1)} %collective-permute-done.3.refs_3_), channel_id=1, source_target_pairs={{0,1},{1,0},{2,3},{3,2},{4,5},{5,4},{6,7},{7,6},{8,9},{9,8},{10,11... | collective-permute-start | bytes 196616 | tf_op jit(solution)/shard_map/ppermute | solution.py:275
  14.4 4.3 %collective-permute-start.7 = (bf16[64,512]{1,0:T(8,128)(2,1)S(1)}, bf16[64,512]{1,0:T(8,128)(2,1)S(1)}, u32[]{:S(2)}, u32[]{:S(2)}) collective-permute-start(bf16[64,512]{1,0:T(8,128)(2,1)S(1)} %get-tuple-element.48), channel_id=1, source_target_pairs={{0,16},{8,24},{16,0},{24,8},{1,17},{9,25},{17,1},{25,9},{2,18},{10... | collective-permute-start | bytes 196616 | tf_op jit(solution)/shard_map/ppermute | solution.py:275
  16.0 5.7 %collective-permute-start.8 = (bf16[64,512]{1,0:T(8,128)(2,1)S(1)}, bf16[64,512]{1,0:T(8,128)(2,1)S(1)}, u32[]{:S(2)}, u32[]{:S(2)}) collective-permute-start(bf16[64,512]{1,0:T(8,128)(2,1)S(1)} %get-tuple-element.49), channel_id=1, source_target_pairs={{0,24},{8,16},{16,8},{24,0},{1,25},{9,17},{17,9},{25,1},{2,26},{10... | collective-permute-start | bytes 196616 | tf_op jit(solution)/shard_map/ppermute | solution.py:275
  17.4 4.3 %collective-permute-start.9 = (bf16[64,512]{1,0:T(8,128)(2,1)S(1)}, bf16[64,512]{1,0:T(8,128)(2,1)S(1)}, u32[]{:S(2)}, u32[]{:S(2)}) collective-permute-start(bf16[64,512]{1,0:T(8,128)(2,1)S(1)} %get-tuple-element.50), channel_id=1, source_target_pairs={{0,8},{8,0},{16,24},{24,16},{1,9},{9,1},{17,25},{25,17},{2,10},{10... | collective-permute-start | bytes 196616 | tf_op jit(solution)/shard_map/ppermute | solution.py:275

commit v4 on v3

--- a/solution.py
+++ b/solution.py
@@ -1,4 +1,5 @@
 import functools
+import math
 
 import jax
 import jax.numpy as jnp
@@ -13,9 +14,10 @@
 GROUP = 8
 
 NEGATIVE = -1e30
+LARGEST = float(np.finfo(np.float32).max)
 EPSILON = 1e-06
 ROPE_BASE = 10000.0
-SCORE_SCALE = 0.125
+SCORE_SCALE = 0.125 * math.log2(math.e)
 F32 = jnp.float32
 BF16 = jnp.bfloat16
 ROWS_BY_ROWS = (((1,), (1,)), ((), ()))
@@ -120,7 +122,7 @@
 
 def queries_kernel(
     pages, page_len, order, normed_ref, table_ref, meta_ref, q_hbm, node_hbm, fill_hbm, out_ref,
-    bias_ref, q_ref, node_ref, fill_ref, sems,
+    limit_ref, q_ref, node_ref, fill_ref, sems,
 ):
     copies = fetch(sems, ((node_hbm, node_ref), (fill_hbm, fill_ref), (q_hbm, q_ref)))
     rows = normed_ref.shape[0]
@@ -129,7 +131,7 @@
     place = me * rows + iota((rows, 128), 0)
     row_start, row_mid, row_leaf = meta_ref[0], meta_ref[1], meta_ref[2]
     width = pages * page_len + rows
-    sources = bias_ref.shape[1] // width
+    sources = limit_ref.shape[1] // width
     copies[0].wait()
     copies[1].wait()
 
@@ -143,8 +145,8 @@
             pieces.append(hit & (slot < fill_ref[number]))
         key_place = block * rows + iota((rows, rows), 1)
         pieces.append((key_place >= row_start[:, :rows]) & (key_place <= place[:, :rows]))
-        bias = jnp.concatenate([jnp.where(ok, 0.0, NEGATIVE) for ok in pieces], axis=1)
-        bias_ref[:, pl.ds(at, width)] = bias
+        limit = jnp.concatenate([jnp.where(ok, LARGEST, NEGATIVE) for ok in pieces], axis=1)
+        limit_ref[:, pl.ds(at, width)] = limit
 
     if order is not None:
         for source, flip in enumerate(order):
@@ -166,23 +168,26 @@
             out_ref[at * rows : (at + 1) * rows, :] = jnp.where(is_key, one, 0.0).astype(BF16)
 
 
-def masked_scores(q_ref, bias_ref, keys, at=0):
-    rows = bias_ref.shape[0]
+def masked_scores(q_ref, limit_ref, keys, at=0):
+    rows = limit_ref.shape[0]
     scores = lax.dot_general(q_ref[...], keys, ROWS_BY_ROWS, preferred_element_type=F32)
     heads, count = q_ref.shape[0] // rows, keys.shape[0]
-    scores = scores.reshape(heads, rows, count) * SCORE_SCALE + bias_ref[:, at : at + count][None]
+    scores = scores.reshape(heads, rows, count) * SCORE_SCALE
+    scores = jnp.minimum(scores, limit_ref[:, at : at + count][None])
     return scores.reshape(heads * rows, count)
 
 
-def fold(scores, keys, state):
+def fold(scores, keys, state, allowed=None):
     top = jnp.max(scores, axis=1, keepdims=True)
     if state is not None:
         top = jnp.maximum(state[0], top)
-    weights = jnp.where(scores > 0.5 * NEGATIVE, jnp.exp(scores - top), 0.0)
+    weights = jnp.exp2(scores - top)
+    if allowed is not None:
+        weights = jnp.where(allowed, weights, 0.0)
     total = jnp.sum(weights, axis=1, keepdims=True)
     accum = jnp.dot(weights.astype(BF16), keys, preferred_element_type=F32)
     if state is not None:
-        factor = jnp.exp(state[0] - top)
+        factor = jnp.exp2(state[0] - top)
         total = total + state[1] * factor
         accum = accum + state[2] * factor
     return top, total, accum
@@ -190,7 +195,7 @@
 
 def project(state, rows, o_ref, outs):
     _, total, accum = state
-    attended = accum / total
+    attended = accum * (1.0 / total)
     second = pltpu.roll(attended, HD, 1)
     is_first = iota((rows, 128), 1) < HD
     parts = []
@@ -217,25 +222,22 @@
     return top[...][:, :1], total[...][:, :1], accum[...]
 
 
-def early_kernel(sources, at, q_ref, bias_ref, *refs):
+def early_kernel(sources, at, q_ref, limit_ref, *refs):
     kv_refs, refs = refs[:sources], refs[sources:]
     keys = jnp.concatenate([ref[...] for ref in kv_refs], axis=0)
     state = load_state(refs[:3]) if at else None
-    state = fold(masked_scores(q_ref, bias_ref, keys, at), keys, state)
+    state = fold(masked_scores(q_ref, limit_ref, keys, at), keys, state)
     store_state(state, refs[-3:])
 
 
-def late_kernel(sources, at, q_ref, bias_ref, o_hbm, *refs):
-    kv_refs, state_refs, rest = refs[:sources], refs[sources : sources + 3], refs[sources + 3 :]
-    *outs, o_ref, sems = rest
-    copies = fetch(sems, ((o_hbm, o_ref),))
+def late_kernel(sources, at, q_ref, limit_ref, o_ref, *refs):
+    kv_refs, state_refs, outs = refs[:sources], refs[sources : sources + 3], refs[sources + 3 :]
     keys = jnp.concatenate([ref[...] for ref in kv_refs], axis=0)
-    state = fold(masked_scores(q_ref, bias_ref, keys, at), keys, load_state(state_refs))
-    copies[0].wait()
-    project(state, bias_ref.shape[0], o_ref, outs)
-
-
-def looped_kernel(steps, q_ref, bias_ref, o_ref, kv_ref, *refs):
+    state = fold(masked_scores(q_ref, limit_ref, keys, at), keys, load_state(state_refs))
+    project(state, limit_ref.shape[0], o_ref, outs)
+
+
+def looped_kernel(steps, q_ref, limit_ref, o_ref, kv_ref, *refs):
     *outs, top_ref, total_ref, accum_ref = refs
     state_refs = (top_ref, total_ref, accum_ref)
     step = pl.program_id(0)
@@ -246,12 +248,14 @@
             ref[...] = jnp.full(ref.shape, value, F32)
 
     keys = kv_ref[...]
-    state = fold(masked_scores(q_ref, bias_ref, keys), keys, load_state(state_refs))
+    scores = masked_scores(q_ref, limit_ref, keys)
+    limit = jnp.concatenate([limit_ref[...]] * (scores.shape[0] // limit_ref.shape[0]), axis=0)
+    state = fold(scores, keys, load_state(state_refs), limit > 0.0)
     store_state(state, state_refs)
 
     @pl.when(step == steps - 1)
     def _():
-        project(load_state(state_refs), bias_ref.shape[0], o_ref, outs)
+        project(load_state(state_refs), limit_ref.shape[0], o_ref, outs)
 
 
 def vmem(count):
@@ -317,7 +321,7 @@
 
     small = blocks == GROUP
     order = (0, 7, 1, 6, 3, 5, 2, 4) if small else None
-    queries, bias = pl.pallas_call(
+    queries, limits = pl.pallas_call(
         functools.partial(queries_kernel, pages, page_len, order),
         out_shape=(shape((heads * rows, 128), BF16), shape((rows, blocks * width))),
         in_specs=vmem(3) + hbm(3),
@@ -348,7 +352,7 @@
                 out_specs=vmem(3),
                 compiler_params=params,
                 cost_estimate=cost(1000, 1000),
-            )(queries, bias, *sources, *state)
+            )(queries, limits, *sources, *state)
             if at == 0:
                 near, *state = lax.optimization_barrier((near, *state))
                 second[2] = near
@@ -356,12 +360,11 @@
         sums = pl.pallas_call(
             functools.partial(late_kernel, len(last), 6 * width),
             out_shape=sums_shape,
-            in_specs=vmem(2) + hbm(1) + vmem(len(last) + 3),
+            in_specs=vmem(6 + len(last)),
             out_specs=vmem(shards),
-            scratch_shapes=[pltpu.VMEM(o_weight.shape, BF16), pltpu.SemaphoreType.DMA((1,))],
             compiler_params=params,
             cost_estimate=cost(1000, 1000),
-        )(queries, bias, o_weight, *last, *state)
+        )(queries, limits, o_weight, *last, *state)
     else:
         gathered = lax.all_gather(own, "blk", axis=0, tiled=True)
         steps = blocks // GROUP
@@ -378,7 +381,7 @@
             out_specs=[pl.BlockSpec((rows, columns), lambda i: (0, 0))] * shards,
             scratch_shapes=[pltpu.VMEM((heads * rows, 128), F32)] * 3,
             compiler_params=params,
-        )(queries, bias, o_weight, gathered)
+        )(queries, limits, o_weight, gathered)
 
     total = sums[0]
     for distance in (2, 3, 1):

time: 22.6 us -> 22.4 us (level)
  Pallas kernels: 5.77 us -> 5.54 us
  transfers between devices with their start and end apart: 10 -> 10, of which waited for: 4 -> 5; matrix products, arithmetic and copies ran while one was open for 0% -> 0% of each run, Pallas kernels for 14% -> 13%
where the time goes in v4:
time: 22.4 us; the launch traced here: 22.3 us
  starting transfers between devices  10.6 us (47%)
  Pallas kernels  5.54 us (25%)
  waiting for transfers between devices  5.39 us (24%)
  other arithmetic  0.66 us (3%)
    ppermute x10, starting transfers between devices, swapped(): lax.ppermute(value, axis, [(device, device ^ distance) for device in rang...  10.6 us
    ppermute x10, waiting for transfers between devices, swapped(): lax.ppermute(value, axis, [(device, device ^ distance) for device in rang...  5.39 us
    pallas_call x1, Pallas kernels, local(): pl.pallas_call(functools.partial(queries_kernel, pages, page_len, order),...  1.71 us
    pallas_call x1, Pallas kernels, local(): pl.pallas_call(keys_kernel, out_shape=(shape((width, 128), BF16), shape(t...  1.61 us
    pallas_call x2, Pallas kernels, local(): pl.pallas_call(functools.partial(early_kernel, len(sources), at), out_sha...  1.26 us
    pallas_call x1, Pallas kernels, local(): pl.pallas_call(functools.partial(late_kernel, len(last), 6 * width), out_...  0.96 us
    convert_element_type x1, other arithmetic, local(): return total.astype(BF16)  0.66 us
  transfers between devices with their start and end apart: 10, of which 5 were waited for; matrix products, arithmetic and copies ran while one was open for 0% of the time, Pallas kernels for 13%

profile of v4, /device:TPU:0, one launch (start us, length us, event | category | flops | bytes accessed | tf_op | source)
XLA Modules:
  0.0 22.3 jit_solution(91839492392737273)
XLA Ops:
  0.0 1.6 %shard_map.118 = (bf16[256,128]{1,0:T(8,128)(2,1)S(1)}, bf16[64,2048]{1,0:T(8,128)(2,1)S(1)}, f32[2,64,128]{2,1,0:T(8,128)S(1)}, s32[3,64,128]{2,1,0:T(8,128)S(1)}) custom-call(f32[1,128]{1,0:T(1,128)} %constant.2.clone.freq_hbm, bf16[64,2048]{1,0:T(8,128)(2,1)} %tokens_hbm.1, bf16[64,2048]{1,0:T(8,128)(2,1)} %bitcast.2, bf16[64,2048]{1,0:T(8,128)(2,1)} %bitcast.3, ...), custom_call_target="tpu_custom_call" | custom-call | tf_op jit(solution)/shard_map/pallas_call | solution.py:302
  1.6 4.6 %collective-permute-start = (bf16[256,128]{1,0:T(8,128)(2,1)S(1)}, bf16[256,128]{1,0:T(8,128)(2,1)S(1)}, u32[]{:S(2)}, u32[]{:S(2)}) collective-permute-start(bf16[256,128]{1,0:T(8,128)(2,1)S(1)} %get-tuple-element.40.refs_0_), channel_id=1, source_target_pairs={{0,7},{1,6},{2,5},{3,4},{4,3},{5,2},{6,1},{7,0},{8,15},{9,14},{10,... | collective-permute-start | bytes 196616 | tf_op jit(solution)/shard_map/ppermute | solution.py:279
  6.2 0.0 collective-permute-start.1
  6.2 0.9 %collective-permute-start.3 = (bf16[256,128]{1,0:T(8,128)(2,1)S(1)}, bf16[256,128]{1,0:T(8,128)(2,1)S(1)}, u32[]{:S(2)}, u32[]{:S(2)}) collective-permute-start(bf16[256,128]{1,0:T(8,128)(2,1)S(1)} %get-tuple-element.40.refs_0_), channel_id=1, source_target_pairs={{0,5},{1,4},{2,7},{3,6},{4,1},{5,0},{6,3},{7,2},{8,13},{9,12},{10,... | collective-permute-start | bytes 196616 | tf_op jit(solution)/shard_map/ppermute | solution.py:279
  7.1 1.7 %shard_map.119 = (bf16[256,128]{1,0:T(8,128)(2,1)S(1)}, f32[64,2048]{1,0:T(8,128)S(1)}) custom-call(bf16[64,2048]{1,0:T(8,128)(2,1)S(1)} %get-tuple-element.29.normed_ref, f32[2,64,128]{2,1,0:T(8,128)S(1)} %get-tuple-element.30.table_ref, s32[3,64,128]{2,1,0:T(8,128)S(1)} %get-tuple-element.31.meta_ref, bf16[2048,256]{1,0:T(8,128)(2,1)} %q_hbm.1, ...), custom_call_target="tpu_custom_call" | custom-call | flops 1000 | bytes 1000 | tf_op jit(solution)/shard_map/pallas_call | solution.py:324
  8.8 0.0 copy-start
  8.8 0.0 collective-permute-done.refs_1_
  8.8 0.7 %collective-permute-start.6 = (bf16[256,128]{1,0:T(8,128)(2,1)S(1)}, bf16[256,128]{1,0:T(8,128)(2,1)S(1)}, u32[]{:S(2)}, u32[]{:S(2)}) collective-permute-start(bf16[256,128]{1,0:T(8,128)(2,1)S(1)} %collective-permute-done.refs_1_), channel_id=1, source_target_pairs={{0,1},{1,0},{2,3},{3,2},{4,5},{5,4},{6,7},{7,6},{8,9},{9,8},{10,11... | collective-permute-start | bytes 196616 | tf_op jit(solution)/shard_map/ppermute | solution.py:279
  9.6 0.0 collective-permute-start.5
  9.6 0.5 %shard_map.120 = (f32[256,128]{1,0:T(8,128)S(1)}, f32[256,128]{1,0:T(8,128)S(1)}, f32[256,128]{1,0:T(8,128)S(1)}) custom-call(bf16[256,128]{1,0:T(8,128)(2,1)S(1)} %get-tuple-element.33.q_ref, f32[64,2048]{1,0:T(8,128)S(1)} %get-tuple-element.34.limit_ref, bf16[256,128]{1,0:T(8,128)(2,1)S(1)} %get-tuple-element.40.refs_0_, ...), custom_call_target="tpu_custom_call" | custom-call | flops 1000 | bytes 1000 | tf_op jit(solution)/shard_map/pallas_call | solution.py:348
  10.0 1.2 %collective-permute-done.1.refs_2_ = bf16[256,128]{1,0:T(8,128)(2,1)S(1)} collective-permute-done((bf16[256,128]{1,0:T(8,128)(2,1)S(1)}, bf16[256,128]{1,0:T(8,128)(2,1)S(1)}, u32[]{:S(2)}, u32[]{:S(2)}) %collective-permute-start.1) | collective-permute-done | bytes 65568 | tf_op jit(solution)/shard_map/ppermute | solution.py:279
  11.2 0.9 %collective-permute-start.2 = (bf16[256,128]{1,0:T(8,128)(2,1)S(1)}, bf16[256,128]{1,0:T(8,128)(2,1)S(1)}, u32[]{:S(2)}, u32[]{:S(2)}) collective-permute-start(bf16[256,128]{1,0:T(8,128)(2,1)S(1)} %collective-permute-done.1.refs_2_), channel_id=1, source_target_pairs={{0,1},{1,0},{2,3},{3,2},{4,5},{5,4},{6,7},{7,6},{8,9},{9,8},{10,11... | collective-permute-start | bytes 196616 | tf_op jit(solution)/shard_map/ppermute | solution.py:279
  12.1 0.0 collective-permute-done.3.refs_3_
  12.1 0.0 collective-permute-start.4
  12.1 0.0 collective-permute-done.6.refs_1_
  12.1 0.0 collective-permute-done.5.refs_0_
  12.1 0.8 %shard_map.121 = (f32[256,128]{1,0:T(8,128)S(1)}, f32[256,128]{1,0:T(8,128)S(1)}, f32[256,128]{1,0:T(8,128)S(1)}) custom-call(bf16[256,128]{1,0:T(8,128)(2,1)S(1)} %get-tuple-element.33.q_ref, f32[64,2048]{1,0:T(8,128)S(1)} %get-tuple-element.34.limit_ref, bf16[256,128]{1,0:T(8,128)(2,1)S(1)} %collective-permute-done.5.refs_0_, ...), custom_call_target="tpu_custom_call" | custom-call | flops 1000 | bytes 1000 | tf_op jit(solution)/shard_map/pallas_call | solution.py:348
  12.9 0.1 collective-permute-done.2.refs_0_
  13.0 0.4 %collective-permute-done.4.refs_1_ = bf16[256,128]{1,0:T(8,128)(2,1)S(1)} collective-permute-done((bf16[256,128]{1,0:T(8,128)(2,1)S(1)}, bf16[256,128]{1,0:T(8,128)(2,1)S(1)}, u32[]{:S(2)}, u32[]{:S(2)}) %collective-permute-start.4) | collective-permute-done | bytes 65568 | tf_op jit(solution)/shard_map/ppermute | solution.py:279
  13.3 0.0 copy-done
  13.3 1.0 %shard_map.122 = (f32[64,512]{1,0:T(8,128)S(1)}, bf16[64,512]{1,0:T(8,128)(2,1)S(1)}, bf16[64,512]{1,0:T(8,128)(2,1)S(1)}, bf16[64,512]{1,0:T(8,128)(2,1)S(1)}) custom-call(bf16[256,128]{1,0:T(8,128)(2,1)S(1)} %get-tuple-element.33.q_ref, f32[64,2048]{1,0:T(8,128)S(1)} %get-tuple-element.34.limit_ref, bf16[256,2048]{1,0:T(8,128)(2,1)S(1)} %copy-done, ...), custom_call_target="tpu_custom_call" | custom-call | flops 1000 | bytes 1000 | tf_op jit(solution)/shard_map/pallas_call | solution.py:360
  14.3 1.6 %collective-permute-start.7 = (bf16[64,512]{1,0:T(8,128)(2,1)S(1)}, bf16[64,512]{1,0:T(8,128)(2,1)S(1)}, u32[]{:S(2)}, u32[]{:S(2)}) collective-permute-start(bf16[64,512]{1,0:T(8,128)(2,1)S(1)} %get-tuple-element.48), channel_id=1, source_target_pairs={{0,16},{8,24},{16,0},{24,8},{1,17},{9,25},{17,1},{25,9},{2,18},{10... | collective-permute-start | bytes 196616 | tf_op jit(solution)/shard_map/ppermute | solution.py:279
  15.9 1.4 %collective-permute-start.8 = (bf16[64,512]{1,0:T(8,128)(2,1)S(1)}, bf16[64,512]{1,0:T(8,128)(2,1)S(1)}, u32[]{:S(2)}, u32[]{:S(2)}) collective-permute-start(bf16[64,512]{1,0:T(8,128)(2,1)S(1)} %get-tuple-element.49), channel_id=1, source_target_pairs={{0,24},{8,16},{16,8},{24,0},{1,25},{9,17},{17,9},{25,1},{2,26},{10... | collective-permute-start | bytes 196616 | tf_op jit(solution)/shard_map/ppermute | solution.py:279
  17.3 0.5 %collective-permute-start.9 = (bf16[64,512]{1,0:T(8,128)(2,1)S(1)}, bf16[64,512]{1,0:T(8,128)(2,1)S(1)}, u32[]{:S(2)}, u32[]{:S(2)}) collective-permute-start(bf16[64,512]{1,0:T(8,128)(2,1)S(1)} %get-tuple-element.50), channel_id=1, source_target_pairs={{0,8},{8,0},{16,24},{24,16},{1,9},{9,1},{17,25},{25,17},{2,10},{10... | collective-permute-start | bytes 196616 | tf_op jit(solution)/shard_map/ppermute | solution.py:279
  17.8 0.8 %collective-permute-done.7 = bf16[64,512]{1,0:T(8,128)(2,1)S(1)} collective-permute-done((bf16[64,512]{1,0:T(8,128)(2,1)S(1)}, bf16[64,512]{1,0:T(8,128)(2,1)S(1)}, u32[]{:S(2)}, u32[]{:S(2)}) %collective-permute-start.7) | collective-permute-done | bytes 65568 | tf_op jit(solution)/shard_map/ppermute | solution.py:279
  18.6 3.0 %collective-permute-done.8 = bf16[64,512]{1,0:T(8,128)(2,1)S(1)} collective-permute-done((bf16[64,512]{1,0:T(8,128)(2,1)S(1)}, bf16[64,512]{1,0:T(8,128)(2,1)S(1)}, u32[]{:S(2)}, u32[]{:S(2)}) %collective-permute-start.8) | collective-permute-done | bytes 65568 | tf_op jit(solution)/shard_map/ppermute | solution.py:279
  21.6 0.0 collective-permute-done.9
  21.6 0.7 %add_convert_fusion = bf16[64,512]{1,0:T(8,128)(2,1)} fusion(bf16[64,512]{1,0:T(8,128)(2,1)S(1)} %collective-permute-done.9, bf16[64,512]{1,0:T(8,128)(2,1)S(1)} %collective-permute-done.8, f32[64,512]{1,0:T(8,128)S(1)} %get-tuple-element.47, bf16[64,512]{1,0:T(8,128)(2,1)S(1)} %collective-permute-done.7), kind=kLoop, calls=%fused_computation | loop fusion | flops 229376 | bytes 393216 | tf_op jit(solution)/shard_map/convert_element_type | solution.py:389
Async XLA Ops:
  1.6 7.2 %collective-permute-start = (bf16[256,128]{1,0:T(8,128)(2,1)S(1)}, bf16[256,128]{1,0:T(8,128)(2,1)S(1)}, u32[]{:S(2)}, u32[]{:S(2)}) collective-permute-start(bf16[256,128]{1,0:T(8,128)(2,1)S(1)} %get-tuple-element.40.refs_0_), channel_id=1, source_target_pairs={{0,7},{1,6},{2,5},{3,4},{4,3},{5,2},{6,1},{7,0},{8,15},{9,14},{10,... | collective-permute-start | bytes 196616 | tf_op jit(solution)/shard_map/ppermute | solution.py:279
  6.2 5.0 %collective-permute-start.1 = (bf16[256,128]{1,0:T(8,128)(2,1)S(1)}, bf16[256,128]{1,0:T(8,128)(2,1)S(1)}, u32[]{:S(2)}, u32[]{:S(2)}) collective-permute-start(bf16[256,128]{1,0:T(8,128)(2,1)S(1)} %get-tuple-element.40.refs_0_), channel_id=1, source_target_pairs={{0,3},{1,2},{2,1},{3,0},{4,7},{5,6},{6,5},{7,4},{8,11},{9,10},{10,... | collective-permute-start | bytes 196616 | tf_op jit(solution)/shard_map/ppermute | solution.py:279
  6.2 5.9 %collective-permute-start.3 = (bf16[256,128]{1,0:T(8,128)(2,1)S(1)}, bf16[256,128]{1,0:T(8,128)(2,1)S(1)}, u32[]{:S(2)}, u32[]{:S(2)}) collective-permute-start(bf16[256,128]{1,0:T(8,128)(2,1)S(1)} %get-tuple-element.40.refs_0_), channel_id=1, source_target_pairs={{0,5},{1,4},{2,7},{3,6},{4,1},{5,0},{6,3},{7,2},{8,13},{9,12},{10,... | collective-permute-start | bytes 196616 | tf_op jit(solution)/shard_map/ppermute | solution.py:279
  8.8 4.5 %copy-start = (bf16[256,2048]{1,0:T(8,128)(2,1)S(1)}, bf16[256,2048]{1,0:T(8,128)(2,1)}, u32[]{:S(2)}) copy-start(bf16[256,2048]{1,0:T(8,128)(2,1)} %o_ref.1) | copy-start | bytes 3145732
  8.8 3.2 %collective-permute-start.6 = (bf16[256,128]{1,0:T(8,128)(2,1)S(1)}, bf16[256,128]{1,0:T(8,128)(2,1)S(1)}, u32[]{:S(2)}, u32[]{:S(2)}) collective-permute-start(bf16[256,128]{1,0:T(8,128)(2,1)S(1)} %collective-permute-done.refs_1_), channel_id=1, source_target_pairs={{0,1},{1,0},{2,3},{3,2},{4,5},{5,4},{6,7},{7,6},{8,9},{9,8},{10,11... | collective-permute-start | bytes 196616 | tf_op jit(solution)/shard_map/ppermute | solution.py:279
  9.6 2.5 %collective-permute-start.5 = (bf16[256,128]{1,0:T(8,128)(2,1)S(1)}, bf16[256,128]{1,0:T(8,128)(2,1)S(1)}, u32[]{:S(2)}, u32[]{:S(2)}) collective-permute-start(bf16[256,128]{1,0:T(8,128)(2,1)S(1)} %get-tuple-element.40.refs_0_), channel_id=1, source_target_pairs={{0,1},{1,0},{2,3},{3,2},{4,5},{5,4},{6,7},{7,6},{8,9},{9,8},{10,11... | collective-permute-start | bytes 196616 | tf_op jit(solution)/shard_map/ppermute | solution.py:279
  11.2 1.8 %collective-permute-start.2 = (bf16[256,128]{1,0:T(8,128)(2,1)S(1)}, bf16[256,128]{1,0:T(8,128)(2,1)S(1)}, u32[]{:S(2)}, u32[]{:S(2)}) collective-permute-start(bf16[256,128]{1,0:T(8,128)(2,1)S(1)} %collective-permute-done.1.refs_2_), channel_id=1, source_target_pairs={{0,1},{1,0},{2,3},{3,2},{4,5},{5,4},{6,7},{7,6},{8,9},{9,8},{10,11... | collective-permute-start | bytes 196616 | tf_op jit(solution)/shard_map/ppermute | solution.py:279
  12.1 1.3 %collective-permute-start.4 = (bf16[256,128]{1,0:T(8,128)(2,1)S(1)}, bf16[256,128]{1,0:T(8,128)(2,1)S(1)}, u32[]{:S(2)}, u32[]{:S(2)}) collective-permute-start(bf16[256,128]{1,0:T(8,128)(2,1)S(1)} %collective-permute-done.3.refs_3_), channel_id=1, source_target_pairs={{0,1},{1,0},{2,3},{3,2},{4,5},{5,4},{6,7},{7,6},{8,9},{9,8},{10,11... | collective-permute-start | bytes 196616 | tf_op jit(solution)/shard_map/ppermute | solution.py:279
  14.3 4.3 %collective-permute-start.7 = (bf16[64,512]{1,0:T(8,128)(2,1)S(1)}, bf16[64,512]{1,0:T(8,128)(2,1)S(1)}, u32[]{:S(2)}, u32[]{:S(2)}) collective-permute-start(bf16[64,512]{1,0:T(8,128)(2,1)S(1)} %get-tuple-element.48), channel_id=1, source_target_pairs={{0,16},{8,24},{16,0},{24,8},{1,17},{9,25},{17,1},{25,9},{2,18},{10... | collective-permute-start | bytes 196616 | tf_op jit(solution)/shard_map/ppermute | solution.py:279
  15.9 5.7 %collective-permute-start.8 = (bf16[64,512]{1,0:T(8,128)(2,1)S(1)}, bf16[64,512]{1,0:T(8,128)(2,1)S(1)}, u32[]{:S(2)}, u32[]{:S(2)}) collective-permute-start(bf16[64,512]{1,0:T(8,128)(2,1)S(1)} %get-tuple-element.49), channel_id=1, source_target_pairs={{0,24},{8,16},{16,8},{24,0},{1,25},{9,17},{17,9},{25,1},{2,26},{10... | collective-permute-start | bytes 196616 | tf_op jit(solution)/shard_map/ppermute | solution.py:279
  17.3 4.3 %collective-permute-start.9 = (bf16[64,512]{1,0:T(8,128)(2,1)S(1)}, bf16[64,512]{1,0:T(8,128)(2,1)S(1)}, u32[]{:S(2)}, u32[]{:S(2)}) collective-permute-start(bf16[64,512]{1,0:T(8,128)(2,1)S(1)} %get-tuple-element.50), channel_id=1, source_target_pairs={{0,8},{8,0},{16,24},{24,16},{1,9},{9,1},{17,25},{25,17},{2,10},{10... | collective-permute-start | bytes 196616 | tf_op jit(solution)/shard_map/ppermute | solution.py:279

commit v5 on v4

--- a/solution.py
+++ b/solution.py
@@ -42,7 +42,7 @@
 
 
 def keys_kernel(
-    freq_hbm, tokens_hbm, k_hbm, v_hbm, pages_hbm, node_hbm, fill_hbm, len_hbm, leaf_hbm,
+    across, freq_hbm, tokens_hbm, k_hbm, v_hbm, pages_hbm, node_hbm, fill_hbm, len_hbm, leaf_hbm,
     parent_hbm, own_ref, normed_ref, table_ref, meta_ref, tokens_ref, kv_ref, node_ref, fill_ref,
     len_ref, leaf_ref, parent_ref, freq_ref, held_ref, sems,
 ):
@@ -74,32 +74,36 @@
         return carry
 
     lax.fori_loop(0, node_ref.shape[0], add_page, 0, unroll=node_ref.shape[0] <= 64)
-    place = lax.axis_index("blk") * rows + iota((rows, 128), 0)
+    me = lax.axis_index("blk")
+    place = me * rows + iota((rows, 128), 0)
+    other = (me ^ across) * rows + iota((rows, 128), 0)
 
     def add_request(request, carry):
-        start, row_start, row_mid, row_leaf, row_prefix = carry
+        start, own_start, own_prefix, row_start, row_mid, row_leaf = carry
         leaf = leaf_ref[request]
         mid_node = 1 + parent_ref[leaf]
         leaf_node = 1 + MIDS + leaf
         prefix = held_ref[0] + held_ref[mid_node] + held_ref[leaf_node]
         reached = place >= start
+        other_reached = other >= start
         return (
             start + len_ref[request],
-            jnp.where(reached, start, row_start),
-            jnp.where(reached, mid_node, row_mid),
-            jnp.where(reached, leaf_node, row_leaf),
-            jnp.where(reached, prefix, row_prefix),
+            jnp.where(reached, start, own_start),
+            jnp.where(reached, prefix, own_prefix),
+            jnp.where(other_reached, start, row_start),
+            jnp.where(other_reached, mid_node, row_mid),
+            jnp.where(other_reached, leaf_node, row_leaf),
         )
 
     zero = jnp.zeros((rows, 128), jnp.int32)
     reqs = len_ref.shape[0]
-    _, row_start, row_mid, row_leaf, row_prefix = lax.fori_loop(
-        0, reqs, add_request, (jnp.int32(0), zero, zero, zero, zero), unroll=reqs <= 8
+    _, own_start, own_prefix, row_start, row_mid, row_leaf = lax.fori_loop(
+        0, reqs, add_request, (jnp.int32(0),) + (zero,) * 5, unroll=reqs <= 8
     )
     meta_ref[0] = row_start
     meta_ref[1] = row_mid
     meta_ref[2] = row_leaf
-    position = row_prefix + (place - row_start)
+    position = own_prefix + (place - own_start)
     angles = position.astype(F32) * freq_ref[...]
     cosine, sine = jnp.cos(angles), jnp.sin(angles)
     table_ref[0] = cosine
@@ -121,14 +125,14 @@
 
 
 def queries_kernel(
-    pages, page_len, order, normed_ref, table_ref, meta_ref, q_hbm, node_hbm, fill_hbm, out_ref,
+    pages, page_len, order, across, normed_ref, table_ref, meta_ref, q_hbm, node_hbm, fill_hbm, out_ref,
     limit_ref, q_ref, node_ref, fill_ref, sems,
 ):
     copies = fetch(sems, ((node_hbm, node_ref), (fill_hbm, fill_ref), (q_hbm, q_ref)))
     rows = normed_ref.shape[0]
     heads = q_ref.shape[1] // HD
     me = lax.axis_index("blk")
-    place = me * rows + iota((rows, 128), 0)
+    place = (me ^ across) * rows + iota((rows, 128), 0)
     row_start, row_mid, row_leaf = meta_ref[0], meta_ref[1], meta_ref[2]
     width = pages * page_len + rows
     sources = limit_ref.shape[1] // width
@@ -299,8 +303,10 @@
     frequency = jnp.asarray(frequency.astype(np.float32).reshape(1, 128))
     params = pltpu.CompilerParams(vmem_limit_bytes=VMEM_LIMIT)
 
+    small = blocks == GROUP
+    across = 1 if small else 0
     own, normed, table, meta = pl.pallas_call(
-        keys_kernel,
+        functools.partial(keys_kernel, across),
         out_shape=(
             shape((width, 128), BF16),
             shape(tokens.shape, BF16),
@@ -319,10 +325,9 @@
         compiler_params=params,
     )(*in_hbm(frequency, tokens, k_weight.T, v_weight.T, kv_pages, *ints))
 
-    small = blocks == GROUP
     order = (0, 7, 1, 6, 3, 5, 2, 4) if small else None
     queries, limits = pl.pallas_call(
-        functools.partial(queries_kernel, pages, page_len, order),
+        functools.partial(queries_kernel, pages, page_len, order, across),
         out_shape=(shape((heads * rows, 128), BF16), shape((rows, blocks * width))),
         in_specs=vmem(3) + hbm(3),
         out_specs=tuple(vmem(2)),
@@ -341,21 +346,16 @@
     if small:
         far, near, middle = (swapped(own, "blk", distance) for distance in (7, 3, 5))
         far, again, queries = lax.optimization_barrier((far, own, queries))
-        first = [own, far]
-        second = [swapped(again, "blk", 1), swapped(far, "blk", 1), near, middle]
-        state = []
-        for sources, at in ((first, 0), (second, 2 * width)):
-            state = pl.pallas_call(
-                functools.partial(early_kernel, len(sources), at),
-                out_shape=state_shape,
-                in_specs=vmem(2 + len(sources) + len(state)),
-                out_specs=vmem(3),
-                compiler_params=params,
-                cost_estimate=cost(1000, 1000),
-            )(queries, limits, *sources, *state)
-            if at == 0:
-                near, *state = lax.optimization_barrier((near, *state))
-                second[2] = near
+        queries = swapped(queries, "blk", 1)
+        direct = [own, far, swapped(own, "blk", 1), swapped(far, "blk", 1), near, middle]
+        state = pl.pallas_call(
+            functools.partial(early_kernel, len(direct), 0),
+            out_shape=state_shape,
+            in_specs=vmem(2 + len(direct)),
+            out_specs=vmem(3),
+            compiler_params=params,
+            cost_estimate=cost(1000, 1000),
+        )(queries, limits, *direct)
         last = [swapped(near, "blk", 1), swapped(middle, "blk", 1)]
         sums = pl.pallas_call(
             functools.partial(late_kernel, len(last), 6 * width),
@@ -383,9 +383,14 @@
             compiler_params=params,
         )(queries, limits, o_weight, gathered)
 
-    total = sums[0]
+    total = swapped(sums[0], "blk", 1) if across else sums[0]
     for distance in (2, 3, 1):
-        total = total + swapped(sums[distance], "head", distance).astype(F32)
+        pairs = [
+            (shard * blocks + block, (shard ^ distance) * blocks + (block ^ across))
+            for shard in range(shards)
+            for block in range(blocks)
+        ]
+        total = total + lax.ppermute(sums[distance], ("head", "blk"), pairs).astype(F32)
     return total.astype(BF16)
 
 

time: 22.4 us -> 22 us (0.982)
  Pallas kernels: 5.54 us -> 5.26 us
    ppermute x0 -> x3, waiting for transfers between devices: none -> 3.53 us  [local(): lax.ppermute(sums[distance], ('head', 'blk'), pairs).astype(F32)]
    ppermute x10 -> x9, waiting for transfers between devices: 5.39 us -> 1.96 us  [swapped(): lax.ppermute(value, axis, [(device, device ^ distance) for device in rang...]
    ppermute x10 -> x9, starting transfers between devices: 10.6 us -> 7.25 us  [swapped(): lax.ppermute(value, axis, [(device, device ^ distance) for device in rang...]
    ppermute x0 -> x3, starting transfers between devices: none -> 3.13 us  [local(): lax.ppermute(sums[distance], ('head', 'blk'), pairs).astype(F32)]
    pallas_call x4 -> x3, Pallas kernels: 4.58 us -> 4.3 us  [the longest x1 1.8 us: local(): pl.pallas_call(functools.partial(queries_kernel, pages, page_len, order,...]
  transfers between devices with their start and end apart: 10 -> 12, of which waited for: 5 -> 5; matrix products, arithmetic and copies ran while one was open for 0% -> 0% of each run, Pallas kernels for 13% -> 12%
where the time goes in v5:
time: 22 us; the launch traced here: 21.9 us
  starting transfers between devices  10.4 us (47%)
  waiting for transfers between devices  5.49 us (25%)
  Pallas kernels  5.26 us (24%)
  other arithmetic  0.66 us (3%)
    ppermute x9, starting transfers between devices, swapped(): lax.ppermute(value, axis, [(device, device ^ distance) for device in rang...  7.25 us
    ppermute x3, waiting for transfers between devices, local(): lax.ppermute(sums[distance], ('head', 'blk'), pairs).astype(F32)  3.53 us
    ppermute x3, starting transfers between devices, local(): lax.ppermute(sums[distance], ('head', 'blk'), pairs).astype(F32)  3.13 us
    ppermute x9, waiting for transfers between devices, swapped(): lax.ppermute(value, axis, [(device, device ^ distance) for device in rang...  1.96 us
    pallas_call x1, Pallas kernels, local(): pl.pallas_call(functools.partial(queries_kernel, pages, page_len, order,...  1.8 us
    pallas_call x1, Pallas kernels, local(): pl.pallas_call(functools.partial(keys_kernel, across), out_shape=(shape((...  1.61 us
    pallas_call x1, Pallas kernels, local(): pl.pallas_call(functools.partial(late_kernel, len(last), 6 * width), out_...  0.96 us
    pallas_call x1, Pallas kernels, local(): pl.pallas_call(functools.partial(early_kernel, len(direct), 0), out_shape...  0.89 us
  transfers between devices with their start and end apart: 12, of which 5 were waited for; matrix products, arithmetic and copies ran while one was open for 0% of the time, Pallas kernels for 12%

profile of v5, /device:TPU:0, one launch (start us, length us, event | category | flops | bytes accessed | tf_op | source)
XLA Modules:
  0.0 21.9 jit_solution(10403172159776222374)
XLA Ops:
  0.0 1.6 %shard_map.118 = (bf16[256,128]{1,0:T(8,128)(2,1)S(1)}, bf16[64,2048]{1,0:T(8,128)(2,1)S(1)}, f32[2,64,128]{2,1,0:T(8,128)S(1)}, s32[3,64,128]{2,1,0:T(8,128)S(1)}) custom-call(f32[1,128]{1,0:T(1,128)} %constant.2.clone.freq_hbm, bf16[64,2048]{1,0:T(8,128)(2,1)} %tokens_hbm.1, bf16[64,2048]{1,0:T(8,128)(2,1)} %bitcast.2, bf16[64,2048]{1,0:T(8,128)(2,1)} %bitcast.3, ...), custom_call_target="tpu_custom_call" | custom-call | tf_op jit(solution)/shard_map/pallas_call | solution.py:308
  1.6 4.6 %collective-permute-start = (bf16[256,128]{1,0:T(8,128)(2,1)S(1)}, bf16[256,128]{1,0:T(8,128)(2,1)S(1)}, u32[]{:S(2)}, u32[]{:S(2)}) collective-permute-start(bf16[256,128]{1,0:T(8,128)(2,1)S(1)} %get-tuple-element.20.refs_0_), channel_id=1, source_target_pairs={{0,7},{1,6},{2,5},{3,4},{4,3},{5,2},{6,1},{7,0},{8,15},{9,14},{10,... | collective-permute-start | bytes 196616 | tf_op jit(solution)/shard_map/ppermute | solution.py:283
  6.2 0.0 collective-permute-start.2
  6.2 0.9 %collective-permute-start.4 = (bf16[256,128]{1,0:T(8,128)(2,1)S(1)}, bf16[256,128]{1,0:T(8,128)(2,1)S(1)}, u32[]{:S(2)}, u32[]{:S(2)}) collective-permute-start(bf16[256,128]{1,0:T(8,128)(2,1)S(1)} %get-tuple-element.20.refs_0_), channel_id=1, source_target_pairs={{0,5},{1,4},{2,7},{3,6},{4,1},{5,0},{6,3},{7,2},{8,13},{9,12},{10,... | collective-permute-start | bytes 196616 | tf_op jit(solution)/shard_map/ppermute | solution.py:283
  7.1 0.0 collective-permute-start.6
  7.1 0.0 copy-start
  7.1 1.8 %shard_map.119 = (bf16[256,128]{1,0:T(8,128)(2,1)S(1)}, f32[64,2048]{1,0:T(8,128)S(1)}) custom-call(bf16[64,2048]{1,0:T(8,128)(2,1)S(1)} %get-tuple-element.21.normed_ref, f32[2,64,128]{2,1,0:T(8,128)S(1)} %get-tuple-element.22.table_ref, s32[3,64,128]{2,1,0:T(8,128)S(1)} %get-tuple-element.23.meta_ref, bf16[2048,256]{1,0:T(8,128)(2,1)} %q_hbm.1, ...), custom_call_target="tpu_custom_call" | custom-call | flops 1000 | bytes 1000 | tf_op jit(solution)/shard_map/pallas_call | solution.py:329
  8.9 0.0 collective-permute-done.refs_1_
  8.9 0.6 %collective-permute-start.1 = (bf16[256,128]{1,0:T(8,128)(2,1)S(1)}, bf16[256,128]{1,0:T(8,128)(2,1)S(1)}, u32[]{:S(2)}, u32[]{:S(2)}) collective-permute-start(bf16[256,128]{1,0:T(8,128)(2,1)S(1)} %get-tuple-element.25), channel_id=1, source_target_pairs={{0,1},{1,0},{2,3},{3,2},{4,5},{5,4},{6,7},{7,6},{8,9},{9,8},{10,11... | collective-permute-start | bytes 196616 | tf_op jit(solution)/shard_map/ppermute | solution.py:283
  9.6 0.0 collective-permute-start.7
  9.6 1.6 %collective-permute-done.2.refs_4_ = bf16[256,128]{1,0:T(8,128)(2,1)S(1)} collective-permute-done((bf16[256,128]{1,0:T(8,128)(2,1)S(1)}, bf16[256,128]{1,0:T(8,128)(2,1)S(1)}, u32[]{:S(2)}, u32[]{:S(2)}) %collective-permute-start.2) | collective-permute-done | bytes 65568 | tf_op jit(solution)/shard_map/ppermute | solution.py:283
  11.2 0.9 %collective-permute-start.3 = (bf16[256,128]{1,0:T(8,128)(2,1)S(1)}, bf16[256,128]{1,0:T(8,128)(2,1)S(1)}, u32[]{:S(2)}, u32[]{:S(2)}) collective-permute-start(bf16[256,128]{1,0:T(8,128)(2,1)S(1)} %collective-permute-done.2.refs_4_), channel_id=1, source_target_pairs={{0,1},{1,0},{2,3},{3,2},{4,5},{5,4},{6,7},{7,6},{8,9},{9,8},{10,11... | collective-permute-start | bytes 196616 | tf_op jit(solution)/shard_map/ppermute | solution.py:283
  12.1 0.0 collective-permute-done.4.refs_5_
  12.1 0.0 collective-permute-start.5
  12.1 0.0 collective-permute-done.6.refs_2_
  12.1 0.0 collective-permute-done.1.q_ref
  12.1 0.0 collective-permute-done.7.refs_3_
  12.1 0.9 %shard_map.120 = (f32[256,128]{1,0:T(8,128)S(1)}, f32[256,128]{1,0:T(8,128)S(1)}, f32[256,128]{1,0:T(8,128)S(1)}) custom-call(bf16[256,128]{1,0:T(8,128)(2,1)S(1)} %collective-permute-done.1.q_ref, f32[64,2048]{1,0:T(8,128)S(1)} %get-tuple-element.26.limit_ref, bf16[256,128]{1,0:T(8,128)(2,1)S(1)} %get-tuple-element.20.refs_0_, ...), custom_call_target="tpu_custom_call" | custom-call | flops 1000 | bytes 1000 | tf_op jit(solution)/shard_map/pallas_call | solution.py:351
  13.0 0.0 collective-permute-done.3.refs_0_
  13.0 0.3 %collective-permute-done.5.refs_1_ = bf16[256,128]{1,0:T(8,128)(2,1)S(1)} collective-permute-done((bf16[256,128]{1,0:T(8,128)(2,1)S(1)}, bf16[256,128]{1,0:T(8,128)(2,1)S(1)}, u32[]{:S(2)}, u32[]{:S(2)}) %collective-permute-start.5) | collective-permute-done | bytes 65568 | tf_op jit(solution)/shard_map/ppermute | solution.py:283
  13.3 0.0 copy-done
  13.3 1.0 %shard_map.121 = (f32[64,512]{1,0:T(8,128)S(1)}, bf16[64,512]{1,0:T(8,128)(2,1)S(1)}, bf16[64,512]{1,0:T(8,128)(2,1)S(1)}, bf16[64,512]{1,0:T(8,128)(2,1)S(1)}) custom-call(bf16[256,128]{1,0:T(8,128)(2,1)S(1)} %collective-permute-done.1.q_ref, f32[64,2048]{1,0:T(8,128)S(1)} %get-tuple-element.26.limit_ref, bf16[256,2048]{1,0:T(8,128)(2,1)S(1)} %copy-done, ...), custom_call_target="tpu_custom_call" | custom-call | flops 1000 | bytes 1000 | tf_op jit(solution)/shard_map/pallas_call | solution.py:360
  14.3 0.3 %collective-permute-start.8 = (f32[64,512]{1,0:T(8,128)S(1)}, f32[64,512]{1,0:T(8,128)S(1)}, u32[]{:S(2)}, u32[]{:S(2)}) collective-permute-start(f32[64,512]{1,0:T(8,128)S(1)} %get-tuple-element.31), channel_id=1, source_target_pairs={{0,1},{1,0},{2,3},{3,2},{4,5},{5,4},{6,7},{7,6},{8,9},{9,8},{10,11... | collective-permute-start | bytes 393224 | tf_op jit(solution)/shard_map/ppermute | solution.py:283
  14.5 2.4 %collective-permute-start.10 = (bf16[64,512]{1,0:T(8,128)(2,1)S(1)}, bf16[64,512]{1,0:T(8,128)(2,1)S(1)}, u32[]{:S(2)}, u32[]{:S(2)}) collective-permute-start(bf16[64,512]{1,0:T(8,128)(2,1)S(1)} %get-tuple-element.33), channel_id=1, source_target_pairs={{0,25},{1,24},{2,27},{3,26},{4,29},{5,28},{6,31},{7,30},{8,17},{9,... | collective-permute-start | bytes 196616 | tf_op jit(solution)/shard_map/ppermute | solution.py:393
  16.9 0.3 %collective-permute-start.11 = (bf16[64,512]{1,0:T(8,128)(2,1)S(1)}, bf16[64,512]{1,0:T(8,128)(2,1)S(1)}, u32[]{:S(2)}, u32[]{:S(2)}) collective-permute-start(bf16[64,512]{1,0:T(8,128)(2,1)S(1)} %get-tuple-element.34), channel_id=1, source_target_pairs={{0,9},{1,8},{2,11},{3,10},{4,13},{5,12},{6,15},{7,14},{8,1},{9,0},... | collective-permute-start | bytes 196616 | tf_op jit(solution)/shard_map/ppermute | solution.py:393
  17.2 0.4 %collective-permute-start.9 = (bf16[64,512]{1,0:T(8,128)(2,1)S(1)}, bf16[64,512]{1,0:T(8,128)(2,1)S(1)}, u32[]{:S(2)}, u32[]{:S(2)}) collective-permute-start(bf16[64,512]{1,0:T(8,128)(2,1)S(1)} %get-tuple-element.32), channel_id=1, source_target_pairs={{0,17},{1,16},{2,19},{3,18},{4,21},{5,20},{6,23},{7,22},{8,25},{9,... | collective-permute-start | bytes 196616 | tf_op jit(solution)/shard_map/ppermute | solution.py:393
  17.7 1.7 %collective-permute-done.10 = bf16[64,512]{1,0:T(8,128)(2,1)S(1)} collective-permute-done((bf16[64,512]{1,0:T(8,128)(2,1)S(1)}, bf16[64,512]{1,0:T(8,128)(2,1)S(1)}, u32[]{:S(2)}, u32[]{:S(2)}) %collective-permute-start.10) | collective-permute-done | bytes 65568 | tf_op jit(solution)/shard_map/ppermute | solution.py:393
  19.4 1.6 %collective-permute-done.11 = bf16[64,512]{1,0:T(8,128)(2,1)S(1)} collective-permute-done((bf16[64,512]{1,0:T(8,128)(2,1)S(1)}, bf16[64,512]{1,0:T(8,128)(2,1)S(1)}, u32[]{:S(2)}, u32[]{:S(2)}) %collective-permute-start.11) | collective-permute-done | bytes 65568 | tf_op jit(solution)/shard_map/ppermute | solution.py:393
  21.0 0.2 collective-permute-done.9
  21.2 0.0 collective-permute-done.8
  21.2 0.7 %add_convert_fusion = bf16[64,512]{1,0:T(8,128)(2,1)} fusion(bf16[64,512]{1,0:T(8,128)(2,1)S(1)} %collective-permute-done.11, bf16[64,512]{1,0:T(8,128)(2,1)S(1)} %collective-permute-done.10, f32[64,512]{1,0:T(8,128)S(1)} %collective-permute-done.8, bf16[64,512]{1,0:T(8,128)(2,1)S(1)} %collective-permute-done.9), kind=kLoop, calls=%fused_computation | loop fusion | flops 229376 | bytes 393216 | tf_op jit(solution)/shard_map/convert_element_type | solution.py:394
Async XLA Ops:
  1.6 7.3 %collective-permute-start = (bf16[256,128]{1,0:T(8,128)(2,1)S(1)}, bf16[256,128]{1,0:T(8,128)(2,1)S(1)}, u32[]{:S(2)}, u32[]{:S(2)}) collective-permute-start(bf16[256,128]{1,0:T(8,128)(2,1)S(1)} %get-tuple-element.20.refs_0_), channel_id=1, source_target_pairs={{0,7},{1,6},{2,5},{3,4},{4,3},{5,2},{6,1},{7,0},{8,15},{9,14},{10,... | collective-permute-start | bytes 196616 | tf_op jit(solution)/shard_map/ppermute | solution.py:283
  6.2 5.0 %collective-permute-start.2 = (bf16[256,128]{1,0:T(8,128)(2,1)S(1)}, bf16[256,128]{1,0:T(8,128)(2,1)S(1)}, u32[]{:S(2)}, u32[]{:S(2)}) collective-permute-start(bf16[256,128]{1,0:T(8,128)(2,1)S(1)} %get-tuple-element.20.refs_0_), channel_id=1, source_target_pairs={{0,3},{1,2},{2,1},{3,0},{4,7},{5,6},{6,5},{7,4},{8,11},{9,10},{10,... | collective-permute-start | bytes 196616 | tf_op jit(solution)/shard_map/ppermute | solution.py:283
  6.2 5.9 %collective-permute-start.4 = (bf16[256,128]{1,0:T(8,128)(2,1)S(1)}, bf16[256,128]{1,0:T(8,128)(2,1)S(1)}, u32[]{:S(2)}, u32[]{:S(2)}) collective-permute-start(bf16[256,128]{1,0:T(8,128)(2,1)S(1)} %get-tuple-element.20.refs_0_), channel_id=1, source_target_pairs={{0,5},{1,4},{2,7},{3,6},{4,1},{5,0},{6,3},{7,2},{8,13},{9,12},{10,... | collective-permute-start | bytes 196616 | tf_op jit(solution)/shard_map/ppermute | solution.py:283
  7.1 5.0 %collective-permute-start.6 = (bf16[256,128]{1,0:T(8,128)(2,1)S(1)}, bf16[256,128]{1,0:T(8,128)(2,1)S(1)}, u32[]{:S(2)}, u32[]{:S(2)}) collective-permute-start(bf16[256,128]{1,0:T(8,128)(2,1)S(1)} %get-tuple-element.20.refs_0_), channel_id=1, source_target_pairs={{0,1},{1,0},{2,3},{3,2},{4,5},{5,4},{6,7},{7,6},{8,9},{9,8},{10,11... | collective-permute-start | bytes 196616 | tf_op jit(solution)/shard_map/ppermute | solution.py:283
  7.1 6.2 %copy-start = (bf16[256,2048]{1,0:T(8,128)(2,1)S(1)}, bf16[256,2048]{1,0:T(8,128)(2,1)}, u32[]{:S(2)}) copy-start(bf16[256,2048]{1,0:T(8,128)(2,1)} %o_ref.1) | copy-start | bytes 3145732
  8.9 3.1 %collective-permute-start.1 = (bf16[256,128]{1,0:T(8,128)(2,1)S(1)}, bf16[256,128]{1,0:T(8,128)(2,1)S(1)}, u32[]{:S(2)}, u32[]{:S(2)}) collective-permute-start(bf16[256,128]{1,0:T(8,128)(2,1)S(1)} %get-tuple-element.25), channel_id=1, source_target_pairs={{0,1},{1,0},{2,3},{3,2},{4,5},{5,4},{6,7},{7,6},{8,9},{9,8},{10,11... | collective-permute-start | bytes 196616 | tf_op jit(solution)/shard_map/ppermute | solution.py:283
  9.6 2.5 %collective-permute-start.7 = (bf16[256,128]{1,0:T(8,128)(2,1)S(1)}, bf16[256,128]{1,0:T(8,128)(2,1)S(1)}, u32[]{:S(2)}, u32[]{:S(2)}) collective-permute-start(bf16[256,128]{1,0:T(8,128)(2,1)S(1)} %collective-permute-done.refs_1_), channel_id=1, source_target_pairs={{0,1},{1,0},{2,3},{3,2},{4,5},{5,4},{6,7},{7,6},{8,9},{9,8},{10,11... | collective-permute-start | bytes 196616 | tf_op jit(solution)/shard_map/ppermute | solution.py:283
  11.2 1.8 %collective-permute-start.3 = (bf16[256,128]{1,0:T(8,128)(2,1)S(1)}, bf16[256,128]{1,0:T(8,128)(2,1)S(1)}, u32[]{:S(2)}, u32[]{:S(2)}) collective-permute-start(bf16[256,128]{1,0:T(8,128)(2,1)S(1)} %collective-permute-done.2.refs_4_), channel_id=1, source_target_pairs={{0,1},{1,0},{2,3},{3,2},{4,5},{5,4},{6,7},{7,6},{8,9},{9,8},{10,11... | collective-permute-start | bytes 196616 | tf_op jit(solution)/shard_map/ppermute | solution.py:283
  12.1 1.3 %collective-permute-start.5 = (bf16[256,128]{1,0:T(8,128)(2,1)S(1)}, bf16[256,128]{1,0:T(8,128)(2,1)S(1)}, u32[]{:S(2)}, u32[]{:S(2)}) collective-permute-start(bf16[256,128]{1,0:T(8,128)(2,1)S(1)} %collective-permute-done.4.refs_5_), channel_id=1, source_target_pairs={{0,1},{1,0},{2,3},{3,2},{4,5},{5,4},{6,7},{7,6},{8,9},{9,8},{10,11... | collective-permute-start | bytes 196616 | tf_op jit(solution)/shard_map/ppermute | solution.py:283
  14.3 6.9 %collective-permute-start.8 = (f32[64,512]{1,0:T(8,128)S(1)}, f32[64,512]{1,0:T(8,128)S(1)}, u32[]{:S(2)}, u32[]{:S(2)}) collective-permute-start(f32[64,512]{1,0:T(8,128)S(1)} %get-tuple-element.31), channel_id=1, source_target_pairs={{0,1},{1,0},{2,3},{3,2},{4,5},{5,4},{6,7},{7,6},{8,9},{9,8},{10,11... | collective-permute-start | bytes 393224 | tf_op jit(solution)/shard_map/ppermute | solution.py:283
  14.5 4.9 %collective-permute-start.10 = (bf16[64,512]{1,0:T(8,128)(2,1)S(1)}, bf16[64,512]{1,0:T(8,128)(2,1)S(1)}, u32[]{:S(2)}, u32[]{:S(2)}) collective-permute-start(bf16[64,512]{1,0:T(8,128)(2,1)S(1)} %get-tuple-element.33), channel_id=1, source_target_pairs={{0,25},{1,24},{2,27},{3,26},{4,29},{5,28},{6,31},{7,30},{8,17},{9,... | collective-permute-start | bytes 196616 | tf_op jit(solution)/shard_map/ppermute | solution.py:393
  16.9 4.1 %collective-permute-start.11 = (bf16[64,512]{1,0:T(8,128)(2,1)S(1)}, bf16[64,512]{1,0:T(8,128)(2,1)S(1)}, u32[]{:S(2)}, u32[]{:S(2)}) collective-permute-start(bf16[64,512]{1,0:T(8,128)(2,1)S(1)} %get-tuple-element.34), channel_id=1, source_target_pairs={{0,9},{1,8},{2,11},{3,10},{4,13},{5,12},{6,15},{7,14},{8,1},{9,0},... | collective-permute-start | bytes 196616 | tf_op jit(solution)/shard_map/ppermute | solution.py:393
  17.2 4.0 %collective-permute-start.9 = (bf16[64,512]{1,0:T(8,128)(2,1)S(1)}, bf16[64,512]{1,0:T(8,128)(2,1)S(1)}, u32[]{:S(2)}, u32[]{:S(2)}) collective-permute-start(bf16[64,512]{1,0:T(8,128)(2,1)S(1)} %get-tuple-element.32), channel_id=1, source_target_pairs={{0,17},{1,16},{2,19},{3,18},{4,21},{5,20},{6,23},{7,22},{8,25},{9,... | collective-permute-start | bytes 196616 | tf_op jit(solution)/shard_map/ppermute | solution.py:393
